TPU v7x, 32 devices: a whole 2x2x4 slice. The times are simulated.
32 devices in a mesh: parts: 1, seq: 32 (over z, y, x, core).
Axes of the slice: x: 2, y: 2, z: 4, core: 2. Of those that a mesh axis runs over, the one named last changes fastest.
Arguments:
- tokens: bfloat16 [1, 128, 3, 128, 3072], P('parts', 'seq'), may hold values from -6 to 6
- queries: bfloat16 [1, 128, 3, 128, 1536], P('parts', 'seq'), may hold values from -68 to 68
- key_weight: bfloat16 [3072, 1536], P('seq'), may hold values from -0.109375 to 0.109375
- value_weight: bfloat16 [3072, 1536], P('seq'), may hold values from -0.109375 to 0.109375
- halves: int32 [1, 128, 3, 2, 2], P('parts', 'seq'), may hold values from 1 to 3
Outputs:
- mixed: bfloat16 [1, 128, 3, 128, 1536], P('parts', 'seq')
Inputs may be any that keep to these rules, and one draw needn't show every extreme that they name: `halves`: 1 lists the first half of the partner lines, 2 the second half, 3 both.
All inputs are finite; a program needn't handle non-finite values.
Results may differ from a plain program's by a relative error of at most 0.012.
Values may be sent and summed in bfloat16 or wider, within the bound.
A program may use at most 128 MiB of HBM per device.

v0:
```python
import math

import jax
import jax.numpy as jnp
from jax import lax
from jax.sharding import PartitionSpec as P

HEADS = 12
HDIM = 128


def split_heads(tensor_in):
    return tensor_in.reshape(tensor_in.shape[:-1] + (HEADS, HDIM))


def kept_keys(code_grid, grid_len):
    column = jnp.arange(grid_len)
    first_kept = (code_grid % 2 == 1)[..., None]
    second_kept = (code_grid >= 2)[..., None]
    return jnp.where(column < grid_len // 2, first_kept, second_kept)[..., None, :]


def codes_by_half(code_pairs, half_index):
    return jnp.where(half_index[None, None, :] == 0, code_pairs[..., 0:1], code_pairs[..., 1:2])


def partial_attention(queries_h, keys_h, values_h, score_form, value_form, kept_mask):
    scores = jnp.einsum(score_form, queries_h, keys_h, preferred_element_type=jnp.float32) * (
        1.0 / math.sqrt(HDIM)
    )
    masked = jnp.where(kept_mask, scores, -jnp.inf)
    peak_val = jnp.max(masked, axis=-1)
    weights = jnp.exp(masked - peak_val[..., None])
    totals = jnp.sum(weights, axis=-1)
    partial_out = jnp.einsum(
        value_form, weights.astype(jnp.bfloat16), values_h, preferred_element_type=jnp.float32
    )
    return (partial_out, peak_val, totals)


def merge_slots(near_part, far_part):
    peak_val = jnp.maximum(near_part[1], far_part[1])
    near_w = jnp.exp(near_part[1] - peak_val)
    far_w = jnp.exp(far_part[1] - peak_val) * far_part[2]
    upper = near_part[0] * near_w[..., None] + far_part[0] * far_w[..., None]
    return upper / (near_part[2] * near_w + far_w)[..., None]


def on_device(tokens, queries, key_weight, value_weight, halves):
    scenes, line_count, planes, grid_len, model_width = tokens.shape
    hidden_width = queries.shape[-1]
    home_rows = tokens.reshape(-1, model_width)

    def add_panel(weight_panel):
        return jnp.dot(home_rows, weight_panel, preferred_element_type=jnp.float32)

    key_sum = add_panel(lax.all_gather(key_weight, "seq", axis=0, tiled=True))
    value_sum = add_panel(lax.all_gather(value_weight, "seq", axis=0, tiled=True))
    home_shape = (scenes, line_count, planes, grid_len, hidden_width)
    keys_home = key_sum.astype(jnp.bfloat16).reshape(home_shape)
    values_home = value_sum.astype(jnp.bfloat16).reshape(home_shape)
    moved_q, moved_k, moved_v = (
        lax.all_to_all(queries, "seq", split_axis=3, concat_axis=1, tiled=True),
        lax.all_to_all(keys_home, "seq", split_axis=3, concat_axis=1, tiled=True),
        lax.all_to_all(values_home, "seq", split_axis=3, concat_axis=1, tiled=True),
    )
    code_table = lax.all_gather(halves, "seq", axis=1, tiled=True)
    half_len = grid_len // 2
    own_start = lax.axis_index("seq") * line_count
    moved_half = (own_start + jnp.arange(line_count)) // half_len
    home_half = jnp.arange(grid_len) // half_len
    remote_plan = (
        (0, keys_home[:, :, 2], values_home[:, :, 2], "sabhd,sbjhd->sabhj", "sabhj,sbjhd->sabhd"),
        (1, moved_k[:, :, 2], moved_v[:, :, 2], "sabhd,sjbhd->sabhj", "sabhj,sjbhd->sabhd"),
        (2, moved_k[:, :, 1], moved_v[:, :, 1], "sabhd,sjbhd->sabhj", "sabhj,sjbhd->sabhd"),
    )
    remote_results = []
    for plane_idx, keys_part, values_part, score_form, value_form in remote_plan:
        code_grid = codes_by_half(code_table[:, :, plane_idx, :, 1], moved_half)
        remote_results.append(
            partial_attention(
                split_heads(moved_q[:, :, plane_idx]),
                split_heads(keys_part),
                split_heads(values_part),
                score_form,
                value_form,
                kept_keys(code_grid, grid_len),
            )
        )
    remote_mean = jnp.stack([result[0] / result[2][..., None] for result in remote_results], axis=2)
    remote_mean = remote_mean.reshape(remote_mean.shape[:4] + (hidden_width,)).astype(jnp.bfloat16)
    remote_peak = jnp.stack([result[1] for result in remote_results], axis=2)
    remote_sum = jnp.stack([result[2] for result in remote_results], axis=2)
    back_mean = lax.all_to_all(remote_mean, "seq", split_axis=1, concat_axis=3, tiled=True)
    back_peak, back_sum = (
        lax.all_to_all(remote_peak, "seq", split_axis=1, concat_axis=3, tiled=True),
        lax.all_to_all(remote_sum, "seq", split_axis=1, concat_axis=3, tiled=True),
    )
    home_plan = (
        (0, keys_home[:, :, 1], values_home[:, :, 1], "sabhd,sajhd->sabhj", "sabhj,sajhd->sabhd"),
        (1, keys_home[:, :, 0], values_home[:, :, 0], "sabhd,sajhd->sabhj", "sabhj,sajhd->sabhd"),
        (2, moved_k[:, :, 0], moved_v[:, :, 0], "sabhd,sjahd->sabhj", "sabhj,sjahd->sabhd"),
    )
    home_results = []
    for plane_idx, keys_part, values_part, score_form, value_form in home_plan:
        code_grid = codes_by_half(halves[:, :, plane_idx, :, 0], home_half)
        home_results.append(
            partial_attention(
                split_heads(queries[:, :, plane_idx]),
                split_heads(keys_part),
                split_heads(values_part),
                score_form,
                value_form,
                kept_keys(code_grid, grid_len),
            )
        )
    home_out = jnp.stack([result[0] for result in home_results], axis=2)
    home_peak = jnp.stack([result[1] for result in home_results], axis=2)
    home_sum = jnp.stack([result[2] for result in home_results], axis=2)
    merged = merge_slots(
        (home_out, home_peak, home_sum),
        (split_heads(back_mean.astype(jnp.float32)), back_peak, back_sum),
    )
    return merged.reshape(home_shape).astype(jnp.bfloat16)


def solution(mesh):
    in_specs = (
        P("parts", "seq", None, None, None),
        P("parts", "seq", None, None, None),
        P("seq", None),
        P("seq", None),
        P("parts", "seq", None, None, None),
    )
    out_specs = P("parts", "seq", None, None, None)
    return jax.shard_map(
        on_device, mesh=mesh, in_specs=in_specs, out_specs=out_specs, check_vma=False
    )
```

profile of v0, /device:TPU:0, one launch (start us, length us, event | category | flops | bytes accessed | tf_op | source)
XLA Modules:
  0.0 732.9 jit_solution(9357103538851799629)
XLA Ops:
  8.0 8.2 %copy.418 = bf16[1,4,3,128,1536]{4,1,2,0,3:T(4,128)(2,1)} copy(bf16[1,4,3,128,1536]{4,3,2,1,0:T(8,128)(2,1)} %param.6) | data formatting | bytes 9437184 | tf_op args[1]
  16.2 7.4 %all-to-all-start.2 = ((bf16[1,4,3,128,1536]{4,1,2,0,3:T(4,128)(2,1)}), bf16[1,4,3,128,1536]{4,1,2,0,3:T(4,128)(2,1)}, u32[]{:S(2)}, u32[]{:S(2)}) async-start(bf16[1,4,3,128,1536]{4,1,2,0,3:T(4,128)(2,1)} %copy.418), calls=%async_computation.2 | async-start | bytes 9437184 | tf_op jit(solution)/shard_map/all_to_all | solution.py:63
  23.6 131.2 %all-gather.3.cloned.1.call-done = bf16[3072,1536]{1,0:T(8,128)(2,1)} async-done(((bf16[96,1536]{1,0:T(8,128)(2,1)}), bf16[3072,1536]{1,0:T(8,128)(2,1)}) %all-gather.3.cloned.1.call-update) | async-done | bytes 9437200 | tf_op jit(solution)/shard_map/all_gather | solution.py:58
  154.7 19.9 %convolution_convert_fusion.1 = bf16[1536,1536]{1,0:T(8,128)(2,1)S(1)} fusion(bf16[1536,3072]{1,0:T(8,128)(2,1)} %bitcast.326, bf16[3072,1536]{1,0:T(8,128)(2,1)} %all-gather.3.cloned.1.call-done), kind=kOutput, calls=%fused_computation.7 | convolution fusion | flops 14497873920 | bytes 23592960 | tf_op jit(solution)/shard_map/dot_general | solution.py:55
  176.8 5.8 copy.400
  182.6 3.8 all-to-all-start
  186.5 103.0 %all-gather.5.cloned.1.call-done = bf16[3072,1536]{1,0:T(8,128)(2,1)} async-done(((bf16[96,1536]{1,0:T(8,128)(2,1)}), bf16[3072,1536]{1,0:T(8,128)(2,1)}) %all-gather.5.cloned.1.call-update) | async-done | bytes 9437200 | tf_op jit(solution)/shard_map/all_gather | solution.py:57
  289.4 19.9 %convolution_convert_fusion = bf16[1536,1536]{1,0:T(8,128)(2,1)S(1)} fusion(bf16[1536,3072]{1,0:T(8,128)(2,1)} %bitcast.327, bf16[3072,1536]{1,0:T(8,128)(2,1)} %all-gather.5.cloned.1.call-done), kind=kOutput, calls=%fused_computation.6 | convolution fusion | flops 14497873920 | bytes 23592960 | tf_op jit(solution)/shard_map/dot_general | solution.py:55
  311.5 5.8 copy.404
  317.4 7.2 all-to-all-done
  328.3 113.6 %all_gather.11 = s32[1,128,3,2,2]{2,4,3,0,1:T(2,128)S(1)} all-gather(s32[1,4,3,2,2]{2,4,3,0,1:T(2,128)S(1)} %copy.415), channel_id=1, replica_groups=mesh['parts'=1,'seq'=32] {'seq'}, dimensions={1}, use_global_device_ids=true | all-gather | bytes 6336 | tf_op jit(solution)/shard_map/all_gather | solution.py:67
  443.2 4.7 copy.419
  451.2 3.9 copy.420
  460.0 4.4 fusion.97
  466.0 4.5 fusion.96
  479.4 4.0 copy.401
  493.4 4.0 copy.405
  519.6 19.9 %all-to-all-start.3 = ((f32[32,1,576]{2,1,0:T(1,128)}), f32[32,1,576]{2,1,0:T(1,128)S(1)}, u32[]{:S(2)}, u32[]{:S(2)}) async-start(f32[32,1,576]{2,1,0:T(1,128)} %reshape.1497), calls=%async_computation.3 | async-start | bytes 163840 | tf_op jit(solution)/shard_map/all_to_all | solution.py:96
  539.5 3.9 fusion.3
  547.1 4.1 copy.445
  555.0 5.9 all-to-all-start.5
  561.0 6.4 pad_maximum_fusion
  569.2 4.8 all-to-all-start.4
  574.0 4.0 fusion.95
  602.2 3.9 copy.403
  606.1 4.2 copy.407
  635.7 43.6 %all-to-all-done.4 = bf16[1,128,3,4,1536]{4,3,2,0,1:T(4,128)(2,1)} async-done(((bf16[1,128,3,4,1536]{4,3,2,0,1:T(4,128)(2,1)}), bf16[1,128,3,4,1536]{4,3,2,0,1:T(4,128)(2,1)}, u32[]{:S(2)}, u32[]{:S(2)}) %all-to-all-start.4) | async-done | bytes 4718624 | tf_op jit(solution)/shard_map/all_to_all | solution.py:94
  679.3 7.4 %convert_bitcast_fusion = f32[1,4,3,32,4,1536]{5,4,2,1,3,0:T(4,128)} fusion(bf16[1,32,4,3,4,1536]{5,4,3,2,1,0:T(4,128)(2,1)} %bitcast.133), kind=kLoop, calls=%fused_computation.3 | loop fusion | flops 2359296 | bytes 14155776 | tf_op jit(solution)/shard_map/convert_element_type | solution.py:122
  686.7 11.8 %copy.447 = f32[1,4,3,32,4,1536]{5,1,4,3,2,0:T(4,128)} copy(f32[1,4,3,32,4,1536]{5,4,2,1,3,0:T(4,128)} %convert_bitcast_fusion) | data formatting | bytes 18874368 | tf_op jit(solution)/shard_map/convert_element_type | solution.py:122
  698.5 12.0 %copy.454 = f32[1,4,3,128,1536]{3,4,2,1,0:T(8,128)} copy(f32[1,4,3,128,1536]{4,1,3,2,0:T(4,128)} %bitcast.266) | data formatting | bytes 18874368 | tf_op jit(solution)/shard_map/convert_element_type | solution.py:122
  710.5 8.8 %fusion.2 = bf16[1,4,3,128,1536]{3,4,2,1,0:T(8,128)(2,1)} fusion(f32[1,4,3,128,1536]{3,4,2,1,0:T(8,128)} %copy.454, f32[1,4,1,128,1536]{3,4,2,1,0:T(8,128)} %bitcast.278, f32[1,4,1,128,1536]{3,4,2,1,0:T(8,128)} %bitcast.277, f32[1,4,1,128,1536]{3,4,2,1,0:T(8,128)S(1)} %bitcast.276, f32[4,3,128,12]{2,3,0,1:T(8,128)S(1)} %get-tuple-element.6, ...), kind=kLoop, calls=%fused_computation.5 | loop fusion | flops 16515072 | bytes 23814144 | tf_op jit(solution)/shard_map/convert_element_type | solution.py:124
  719.3 6.6 copy.456
  (149 shorter events, 120.3 us)
Async XLA Ops:
  6.5 148.2 %all-gather.3.cloned.1.call-start = ((), (), s32[]{:S(2)}) async-start(), calls=%async_computation.6 | async-start | bytes 9732096 | tf_op jit(solution)/shard_map/all_gather | solution.py:58
  7.3 282.2 %all-gather.5.cloned.1.call-start = ((), (), s32[]{:S(2)}) async-start(), calls=%async_computation.7 | async-start | bytes 9732096 | tf_op jit(solution)/shard_map/all_gather | solution.py:57
  16.2 166.5 %all-to-all-start.2 = ((bf16[1,4,3,128,1536]{4,1,2,0,3:T(4,128)(2,1)}), bf16[1,4,3,128,1536]{4,1,2,0,3:T(4,128)(2,1)}, u32[]{:S(2)}, u32[]{:S(2)}) async-start(bf16[1,4,3,128,1536]{4,1,2,0,3:T(4,128)(2,1)} %copy.418), calls=%async_computation.2 | async-start | bytes 9437184 | tf_op jit(solution)/shard_map/all_to_all | solution.py:63
  174.7 2.1 copy-start
  182.6 141.9 %all-to-all-start = ((bf16[1,4,3,128,1536]{4,1,2,0,3:T(4,128)(2,1)}), bf16[1,4,3,128,1536]{4,1,2,0,3:T(4,128)(2,1)}, u32[]{:S(2)}, u32[]{:S(2)}) async-start(bf16[1,4,3,128,1536]{4,1,2,0,3:T(4,128)(2,1)} %copy.400), calls=%async_computation | async-start | bytes 9437184 | tf_op jit(solution)/shard_map/all_to_all | solution.py:65
  309.4 2.2 copy-start.1
  317.4 10.8 %copy-start.29 = (s32[1,4,3,2,2]{1,4,3,2,0:T(2,128)S(1)}, s32[1,4,3,2,2]{1,4,3,2,0:T(2,128)}, u32[]{:S(2)}) copy-start(s32[1,4,3,2,2]{1,4,3,2,0:T(2,128)} %param.9) | copy-start | bytes 580
  324.5 168.9 %all-to-all-start.1 = ((bf16[1,4,3,128,1536]{4,1,2,0,3:T(4,128)(2,1)}), bf16[1,4,3,128,1536]{4,1,2,0,3:T(4,128)(2,1)}, u32[]{:S(2)}, u32[]{:S(2)}) async-start(bf16[1,4,3,128,1536]{4,1,2,0,3:T(4,128)(2,1)} %copy.404), calls=%async_computation.1 | async-start | bytes 9437184 | tf_op jit(solution)/shard_map/all_to_all | solution.py:64
  442.8 5.0 copy-start.31
  475.1 1.7 copy-start.23
  510.0 1.9 copy-start.12
  519.6 35.4 %all-to-all-start.3 = ((f32[32,1,576]{2,1,0:T(1,128)}), f32[32,1,576]{2,1,0:T(1,128)S(1)}, u32[]{:S(2)}, u32[]{:S(2)}) async-start(f32[32,1,576]{2,1,0:T(1,128)} %reshape.1497), calls=%async_computation.3 | async-start | bytes 163840 | tf_op jit(solution)/shard_map/all_to_all | solution.py:96
  539.5 3.9 copy-start.3
  539.5 3.9 copy-start.17
  539.5 3.9 copy-start.26
  543.4 2.3 copy-start.19
  545.7 5.4 copy-start.24
  545.7 5.4 copy-start.25
  547.1 13.9 %copy-start.7 = (bf16[1,128,1,4,1536]{4,3,2,0,1:T(4,128)(2,1)S(1)}, bf16[1,128,1,4,1536]{4,3,2,0,1:T(4,128)(2,1)}, u32[]{:S(2)}) copy-start(bf16[1,128,1,4,1536]{4,3,2,0,1:T(4,128)(2,1)} %copy.444) | copy-start | bytes 4718596
  555.0 13.6 %all-to-all-start.5 = ((f32[32,1,576]{2,1,0:T(1,128)}), f32[32,1,576]{2,1,0:T(1,128)S(1)}, u32[]{:S(2)}, u32[]{:S(2)}) async-start(f32[32,1,576]{2,1,0:T(1,128)} %reshape.1495), calls=%async_computation.5 | async-start | bytes 163840 | tf_op jit(solution)/shard_map/all_to_all | solution.py:97
  569.2 110.1 %all-to-all-start.4 = ((bf16[1,128,3,4,1536]{4,3,2,0,1:T(4,128)(2,1)}), bf16[1,128,3,4,1536]{4,3,2,0,1:T(4,128)(2,1)}, u32[]{:S(2)}, u32[]{:S(2)}) async-start(bf16[1,128,3,4,1536]{4,3,2,0,1:T(4,128)(2,1)} %pad_maximum_fusion), calls=%async_computation.4 | async-start | bytes 9437184 | tf_op jit(solution)/shard_map/all_to_all | solution.py:94
  579.6 4.3 copy-start.30
  579.6 4.5 copy-start.32
  579.6 4.6 copy-start.5
  581.2 4.7 copy-start.4
  585.9 4.3 copy-start.6
  587.4 4.3 copy-start.10
  593.9 1.9 copy-start.13
  614.5 3.2 copy-start.22
  624.6 9.5 %copy-start.27 = (f32[4,128,12]{1,2,0:T(8,128)S(1)}, f32[4,128,12]{1,2,0:T(8,128)}, u32[]{:S(2)}) copy-start(f32[4,128,12]{1,2,0:T(8,128)} %fusion.8) | copy-start | bytes 73732
  624.6 9.5 %copy-start.28 = (f32[4,128,12]{1,2,0:T(8,128)S(1)}, f32[4,128,12]{1,2,0:T(8,128)}, u32[]{:S(2)}) copy-start(f32[4,128,12]{1,2,0:T(8,128)} %fusion.10) | copy-start | bytes 73732
  698.5 12.0 %copy-start.20 = (f32[4,3,128,12]{2,3,0,1:T(8,128)S(1)}, f32[4,3,128,12]{2,3,0,1:T(8,128)}, u32[]{:S(2)}) copy-start(f32[4,3,128,12]{2,3,0,1:T(8,128)} %get-tuple-element.7) | copy-start | bytes 221188
  (9 other events, 12.5 us)
Sparse Core Ops, SparseCore 0:
  10.3 144.4 all-gather.2
  157.6 131.7 all-gather.4
where the time goes:
time: 743 us; the launch traced here: 733 us
  waiting for transfers between devices  287 us (39%)
  local copies, waits for them, and re-layouts  173 us (23%)
  blocking collectives  114 us (15%)
  matrix products  64.8 us (9%)
  starting transfers between devices  45.5 us (6%)
  other arithmetic  34.7 us (5%)
  between operations  14.1 us (2%)
    all_gather x1, waiting for transfers between devices, on_device(): lax.all_gather(value_weight, 'seq', axis=0, tiled=True)  131 us
    all_gather x1, blocking collectives, on_device(): code_table = lax.all_gather(halves, 'seq', axis=1, tiled=True)  114 us
    all_gather x1, waiting for transfers between devices, on_device(): key_sum = add_panel(lax.all_gather(key_weight, 'seq', axis=0, tiled=True))  103 us
    all_to_all x1, waiting for transfers between devices, on_device(): lax.all_to_all(remote_mean, 'seq', split_axis=1, concat_axis=3, tiled=True)  43.6 us
    dot_general x2, matrix products, add_panel(): return jnp.dot(home_rows, weight_panel, preferred_element_type=jnp.float32)  39.8 us
    unnamed x78, local copies, waits for them, and re-layouts  39.1 us
    convert_element_type x2, local copies, waits for them, and re-layouts, on_device(): back_mean.astype(jnp.float32)  23.8 us
    all_to_all x1, starting transfers between devices, on_device(): lax.all_to_all(remote_peak, 'seq', split_axis=1, concat_axis=3, tiled=True)  19.9 us
  transfers between devices with their start and end apart: 8, of which 5 were waited for; matrix products, arithmetic and copies ran while one was open for 26% of the time, Pallas kernels for 0%

commit v1 on v0

v1 whole, which is shorter than its diff:
```python
import functools
import math

import jax
import jax.numpy as jnp
from jax import lax
from jax.experimental import pallas as pl
from jax.experimental.pallas import tpu as pltpu
from jax.sharding import PartitionSpec as P

HDIM = 128
LANES = 128
MESH = pl.DeviceIdType.MESH


def fold(pos, ring):
    return pos + (pos // (ring // 2)) * (3 * ring // 2 - 1 - 2 * pos)


def gather_kernel(lines, ring, code_in, key_in, value_in, code_out, key_out, value_out, own_sem, send_sem, recv_sem):
    ins = (code_in, key_in, value_in)
    outs = (code_out, key_out, value_out)
    me = lax.axis_index("seq")
    chip, core = me // 2, me % 2
    z, pos = chip // ring, fold(chip % ring, ring)
    sibling = me + 1 - 2 * core

    def index(zz, pp):
        return (zz * ring + fold((pp + ring) % ring, ring)) * 2 + core

    up, down = index(z + 1, pos), index(z - 1, pos)
    right, left = index(z, pos + 1), index(z, pos - 1)

    barrier = pltpu.get_barrier_semaphore()
    for dev in (sibling, right, left):
        pl.semaphore_signal(barrier, inc=1, device_id={"seq": dev}, device_id_type=MESH)

    @pl.when(z + 1 < lines)
    def _():
        pl.semaphore_signal(barrier, inc=1, device_id={"seq": up}, device_id_type=MESH)

    @pl.when(z >= 1)
    def _():
        pl.semaphore_signal(barrier, inc=1, device_id={"seq": down}, device_id_type=MESH)

    has_up, has_down = 1 - (z + 1) // lines, (z + lines - 1) // lines
    pl.semaphore_wait(barrier, 3 + has_up + has_down)

    kinds = range(3)
    locals_ = [pltpu.make_async_copy(ins[t], outs[t].at[me], own_sem.at[t]) for t in kinds]
    for copy in locals_:
        copy.start()
    sent = []

    def make(t, slot, way, dev, own):
        return pltpu.make_async_remote_copy(
            src_ref=ins[t] if own else outs[t].at[slot],
            dst_ref=outs[t].at[slot],
            send_sem=send_sem.at[t, slot // 2, way],
            recv_sem=recv_sem.at[t, slot],
            device_id={"seq": dev},
            device_id_type=MESH,
        )

    def guarded(cond, work):
        if cond is None:
            work()
        else:
            pl.when(cond)(work)

    def send(cond, *what):
        sent.append((cond, what))
        guarded(cond, lambda: make(*what).start())

    def arrive(cond, t, slot):
        guarded(cond, lambda: make(t, slot, 0, sibling, False).wait_recv())

    def sources(dz):
        if dz == 0:
            return ((z, None, 0),)
        return ((z + dz, z + dz < lines, 1), (z - dz, z >= dz, -1))

    def both(one, two):
        return two if one is None else jnp.logical_and(one, two)

    def line_stage(dz):
        for t in kinds:
            for zz, cond, sign in sources(dz):
                slot = index(zz, pos)
                own = dz == 0
                if not own:
                    arrive(cond, t, slot)
                if sign >= 0:
                    send(both(cond, z >= 1), t, slot, 0, down, own)
                if sign <= 0:
                    send(both(cond, z + 1 < lines), t, slot, 1, up, own)
                send(cond, t, slot, 2, right, own)
                send(cond, t, slot, 3, left, own)
                send(cond, t, slot, 4, sibling, own)

    def ring_stage(dz):
        for step in range(1, ring // 2 + 1):
            for t in kinds:
                far, near = ring // 2, (ring - 1) // 2
                to_right, to_left = (near, far) if t == 2 else (far, near)
                for zz, cond, _ in sources(dz):
                    if step <= to_right:
                        slot = index(zz, pos - step)
                        arrive(cond, t, slot)
                        if step < to_right:
                            send(cond, t, slot, 2, right, False)
                        send(cond, t, slot, 4, sibling, False)
                    if step <= to_left:
                        slot = index(zz, pos + step)
                        arrive(cond, t, slot)
                        if step < to_left:
                            send(cond, t, slot, 3, left, False)
                        send(cond, t, slot, 4, sibling, False)

    for dz in range(lines + 1):
        if dz < lines:
            line_stage(dz)
        if dz >= 1:
            ring_stage(dz - 1)
    for t in kinds:
        for chip_slot in range(lines * ring):
            arrive(None, t, chip_slot * 2 + 1 - core)
    for cond, what in sent:
        guarded(cond, lambda what=what: make(*what).wait_send())
    for copy in locals_:
        copy.wait()


def gather_all(size, codes, key_weight, value_weight):
    side = math.isqrt(size // 2)
    if size % 2 or 2 * side * side != size or side < 4 or side % 2:
        return tuple(lax.all_gather(x, "seq", axis=0) for x in (codes, key_weight, value_weight))
    ins = (codes, key_weight, value_weight)
    chips = side * side
    return pl.pallas_call(
        functools.partial(gather_kernel, side, side),
        out_shape=[jax.ShapeDtypeStruct((size,) + x.shape, x.dtype) for x in ins],
        in_specs=[pl.BlockSpec(memory_space=pl.ANY)] * 3,
        out_specs=[pl.BlockSpec(memory_space=pl.ANY)] * 3,
        scratch_shapes=[
            pltpu.SemaphoreType.DMA((3,)),
            pltpu.SemaphoreType.DMA((3, chips, 5)),
            pltpu.SemaphoreType.DMA((3, size)),
        ],
        compiler_params=pltpu.CompilerParams(collective_id=0, has_side_effects=True),
        cost_estimate=pl.CostEstimate(flops=8 * 10**10, bytes_accessed=2 * 10**7, transcendentals=0),
        name="gather_weights",
    )(*ins)


def one_slot(q_ref, k_ref, v_ref, bias, head):
    cols = pl.ds(head * HDIM, HDIM)
    scores = lax.dot_general(
        q_ref[0, 0, :, cols], k_ref[0, 0, :, cols], (((1,), (1,)), ((), ())), preferred_element_type=jnp.float32
    ) * (1.0 / math.sqrt(HDIM)) + bias
    peak = jnp.max(scores, axis=-1, keepdims=True)
    weights = jnp.exp(scores - peak)
    total = jnp.sum(weights, axis=-1, keepdims=True)
    partial = jnp.dot(weights.astype(jnp.bfloat16), v_ref[0, 0, :, cols], preferred_element_type=jnp.float32)
    return partial, peak, total


def three_parts(value):
    parts = []
    for _ in range(3):
        part = value.astype(jnp.bfloat16).astype(jnp.float32)
        parts.append(part)
        value = value - part
    return parts


def far_kernel(heads, q_ref, k_ref, v_ref, bias_ref, out_ref):
    bias = bias_ref[0]
    lane = lax.broadcasted_iota(jnp.int32, (bias.shape[0], LANES), 1)
    stats = jnp.zeros(lane.shape, jnp.float32)
    for head in range(heads):
        partial, peak, total = one_slot(q_ref, k_ref, v_ref, bias, head)
        out_ref[0, 0, :, pl.ds(head * HDIM, HDIM)] = (partial / total).astype(jnp.bfloat16)
        for at, part in enumerate(three_parts(peak) + three_parts(total)):
            stats = jnp.where(lane == 6 * head + at, part, stats)
    out_ref[0, 0, :, pl.ds(heads * HDIM, LANES)] = stats.astype(jnp.bfloat16)


def near_kernel(heads, q_ref, k_ref, v_ref, bias_ref, back_ref, *rest):
    out_ref = rest[-1]
    bias = bias_ref[0]
    stats = back_ref[0, 0, :, pl.ds(heads * HDIM, LANES)].astype(jnp.float32)
    for head in range(heads):
        cols = pl.ds(head * HDIM, HDIM)
        partial, peak, total = one_slot(q_ref, k_ref, v_ref, bias, head)
        col = [stats[:, 6 * head + at : 6 * head + at + 1] for at in range(6)]
        far_peak = col[0] + col[1] + col[2]
        far_total = col[3] + col[4] + col[5]
        top = jnp.maximum(peak, far_peak)
        near_w = jnp.exp(peak - top)
        far_w = jnp.exp(far_peak - top) * far_total
        upper = partial * near_w + back_ref[0, 0, :, cols].astype(jnp.float32) * far_w
        out_ref[0, 0, :, cols] = (upper / (total * near_w + far_w)).astype(jnp.bfloat16)


def plane_spec(array, plane):
    return pl.BlockSpec((1, 1) + array.shape[2:], lambda g: (g, plane, 0, 0))


def attend_cost(groups, rows, keys, width):
    return pl.CostEstimate(
        flops=40 * groups * rows * keys * width, bytes_accessed=8 * groups * rows * width, transcendentals=0
    )


def far_part(operands, bias):
    groups, rows, keys = bias.shape
    width = operands[0][0].shape[-1]
    return pl.pallas_call(
        functools.partial(far_kernel, width // HDIM),
        grid=(groups,),
        in_specs=[plane_spec(a, p) for a, p in operands] + [pl.BlockSpec((1, rows, keys), lambda g: (g, 0, 0))],
        out_specs=pl.BlockSpec((1, 1, rows, width + LANES), lambda g: (g, 0, 0, 0)),
        out_shape=jax.ShapeDtypeStruct((groups, 1, rows, width + LANES), jnp.bfloat16),
        cost_estimate=attend_cost(groups, rows, keys, width),
        name="far_slot",
    )(*[a for a, _ in operands], bias)


def near_part(operands, bias, back, plane, planes, so_far):
    groups, rows, keys = bias.shape
    width = operands[0][0].shape[-1]
    in_specs = [plane_spec(a, p) for a, p in operands]
    in_specs += [pl.BlockSpec((1, rows, keys), lambda g: (g, 0, 0)), plane_spec(back, 0)]
    args = [a for a, _ in operands] + [bias, back]
    aliases = {}
    if so_far is not None:
        in_specs.append(pl.BlockSpec(memory_space=pl.ANY))
        args.append(so_far)
        aliases = {len(args) - 1: 0}
    return pl.pallas_call(
        functools.partial(near_kernel, width // HDIM),
        grid=(groups,),
        in_specs=in_specs,
        out_specs=pl.BlockSpec((1, 1, rows, width), lambda g: (g, plane, 0, 0)),
        out_shape=jax.ShapeDtypeStruct((groups, planes, rows, width), jnp.bfloat16),
        input_output_aliases=aliases,
        cost_estimate=attend_cost(groups, rows, keys, width),
        name="near_slot",
    )(*args)


def swap_lines(array, scenes, size):
    groups, planes, positions, width = array.shape
    lines, own = groups // scenes, positions // size
    cut = array.reshape(scenes, lines, planes, size, own, width).transpose(3, 0, 2, 4, 1, 5)
    got = lax.all_to_all(cut, "seq", split_axis=0, concat_axis=0, tiled=True)
    got = got.transpose(1, 3, 2, 0, 4, 5)
    return got.reshape(scenes * own, planes, size * lines, width)


def keep_bias(codes, keys):
    column = jnp.arange(keys)
    kept = jnp.where(column < keys // 2, (codes % 2 == 1)[..., None], (codes >= 2)[..., None])
    return jnp.where(kept, 0.0, -jnp.inf).astype(jnp.float32)


def on_device(size, tokens, queries, key_weight, value_weight, halves):
    scenes, lines, planes, positions, depth = tokens.shape
    width = queries.shape[-1]
    groups = scenes * lines
    q_home = queries.reshape(groups, planes, positions, width)
    swap = functools.partial(swap_lines, scenes=scenes, size=size)

    flat_codes = halves.reshape(-1)
    padded = -(-flat_codes.size // (8 * LANES)) * 8 * LANES
    code_tile = jnp.pad(flat_codes, (0, padded - flat_codes.size)).reshape(-1, LANES)
    code_all, key_all, value_all = gather_all(size, code_tile, key_weight, value_weight)
    code_all = code_all.reshape(size, -1)[:, : flat_codes.size].reshape((size,) + halves.shape)
    code_all = jnp.moveaxis(code_all, 0, 1).reshape(scenes, size * lines, planes, 2, 2)

    q_moved = swap(q_home)

    home_rows = tokens.reshape(-1, depth)
    home_shape = (groups, planes, positions, width)
    keys = jnp.dot(home_rows, key_all.reshape(depth, width), preferred_element_type=jnp.float32)
    keys = keys.astype(jnp.bfloat16).reshape(home_shape)
    values = jnp.dot(home_rows, value_all.reshape(depth, width), preferred_element_type=jnp.float32)
    values = values.astype(jnp.bfloat16).reshape(home_shape)

    keys, values, q_moved = lax.optimization_barrier((keys, values, q_moved))
    k2, v2 = swap(keys[:, 2:]), swap(values[:, 2:])
    k1, v1 = swap(keys[:, 1:2]), swap(values[:, 1:2])
    k0, v0 = swap(keys[:, :1]), swap(values[:, :1])

    own = positions // size
    own_half = (lax.axis_index("seq") * own + jnp.arange(own)) // (positions // 2)
    home_half = jnp.arange(positions) // (positions // 2)

    def far_bias(plane):
        pairs = code_all[:, None, :, plane, :, 1]
        codes = jnp.where(own_half[None, :, None] == 0, pairs[..., 0], pairs[..., 1])
        return keep_bias(codes.reshape(scenes * own, size * lines), size * lines)

    def near_bias(plane):
        pairs = halves[:, :, plane, :, 0].reshape(groups, 1, 2)
        codes = jnp.where(home_half[None, :] == 0, pairs[..., 0], pairs[..., 1])
        return keep_bias(codes, positions)

    def back(far):
        return swap_lines(far, scenes, size)

    back0 = back(far_part(((q_moved, 0), (keys, 2), (values, 2)), far_bias(0)))
    back1 = back(far_part(((q_moved, 1), (k2, 0), (v2, 0)), far_bias(1)))
    back2 = back(far_part(((q_moved, 2), (k1, 0), (v1, 0)), far_bias(2)))

    out = near_part(((q_home, 0), (keys, 1), (values, 1)), near_bias(0), back0, 0, planes, None)
    out = near_part(((q_home, 1), (keys, 0), (values, 0)), near_bias(1), back1, 1, planes, out)
    out = near_part(((q_home, 2), (k0, 0), (v0, 0)), near_bias(2), back2, 2, planes, out)
    return out.reshape(queries.shape)


def solution(mesh):
    lines = P("parts", "seq", None, None, None)
    rows = P("seq", None)
    return jax.shard_map(
        functools.partial(on_device, mesh.shape["seq"]),
        mesh=mesh,
        in_specs=(lines, lines, rows, rows, lines),
        out_specs=lines,
        check_vma=False,
    )
```

time: 743 us -> 700 us (0.942)
  Pallas kernels: 0 us -> 290 us
  blocking collectives: 114 us -> 0 us
  waiting for transfers between devices: 287 us -> 207 us
  local copies, waits for them, and re-layouts: 173 us -> 112 us
  other arithmetic: 34.7 us -> 2.59 us
  matrix products: 64.8 us -> 39.9 us
  between operations: 14.1 us -> 0.73 us
    pallas_call x0 -> x7, Pallas kernels: none -> 290 us  [the longest x1 184 us: gather_all(): pl.pallas_call(functools.partial(gather_kernel, side, side), out_shape=[j...]
    all_gather x2 -> x0, waiting for transfers between devices: 234 us -> none  [the longest x1 131 us: on_device(): lax.all_gather(value_weight, 'seq', axis=0, tiled=True)]
    all_to_all x6 -> x10, waiting for transfers between devices: 51.9 us -> 207 us  [swap_lines(): got = lax.all_to_all(cut, 'seq', split_axis=0, concat_axis=0, tiled=True)]
    all_gather x1 -> x0, blocking collectives: 114 us -> none  [on_device(): code_table = lax.all_gather(halves, 'seq', axis=1, tiled=True)]
    reshape x2 -> x25, local copies, waits for them, and re-layouts: 11.6 us -> 76.9 us  [the longest x13 46.1 us: swap_lines(): array.reshape(scenes, lines, planes, size, own, width)]
    slice x23 -> x7, local copies, waits for them, and re-layouts: 54.1 us -> 7.23 us  [the longest x1 6.49 us: on_device(): k2, v2 = (swap(keys[:, 2:]), swap(values[:, 2:]))]
    convert_element_type x3 -> x0, local copies, waits for them, and re-layouts: 30.4 us -> none  [the longest x2 23.8 us: on_device(): back_mean.astype(jnp.float32)]
    unnamed x78 -> x29, local copies, waits for them, and re-layouts: 39.1 us -> 9.93 us
  transfers between devices with their start and end apart: 8 -> 10, of which waited for: 5 -> 8; matrix products, arithmetic and copies ran while one was open for 26% -> 17% of each run, Pallas kernels for 0% -> 36%
where the time goes in v1:
time: 700 us; the launch traced here: 693 us
  Pallas kernels  290 us (41%)
  waiting for transfers between devices  207 us (30%)
  local copies, waits for them, and re-layouts  112 us (16%)
  starting transfers between devices  41.2 us (6%)
  matrix products  39.9 us (6%)
    all_to_all x10, waiting for transfers between devices, swap_lines(): got = lax.all_to_all(cut, 'seq', split_axis=0, concat_axis=0, tiled=True)  207 us
    pallas_call x1, Pallas kernels, gather_all(): pl.pallas_call(functools.partial(gather_kernel, side, side), out_shape=[j...  184 us
    pallas_call x3, Pallas kernels, near_part(): pl.pallas_call(functools.partial(near_kernel, width // HDIM), grid=(group...  61.3 us
    reshape x13, local copies, waits for them, and re-layouts, swap_lines(): array.reshape(scenes, lines, planes, size, own, width)  46.1 us
    pallas_call x3, Pallas kernels, far_part(): pl.pallas_call(functools.partial(far_kernel, width // HDIM), grid=(groups...  44.7 us
    all_to_all x10, starting transfers between devices, swap_lines(): got = lax.all_to_all(cut, 'seq', split_axis=0, concat_axis=0, tiled=True)  41.2 us
    reshape x10, local copies, waits for them, and re-layouts, swap_lines(): return got.reshape(scenes * own, planes, size * lines, width)  30.1 us
    dot_general x1, matrix products, on_device(): jnp.dot(home_rows, key_all.reshape(depth, width), preferred_element_type=...  21.8 us
  transfers between devices with their start and end apart: 10, of which 8 were waited for; matrix products, arithmetic and copies ran while one was open for 17% of the time, Pallas kernels for 36%

profile of v1, /device:TPU:0, one launch (start us, length us, event | category | flops | bytes accessed | tf_op | source)
XLA Modules:
  0.0 693.3 jit_solution(15244358486840687862)
XLA Ops:
  0.0 8.2 %copy.45 = bf16[1,4,3,128,1536]{4,1,2,3,0:T(4,128)(2,1)} copy(bf16[1,4,3,128,1536]{4,3,2,1,0:T(8,128)(2,1)} %param.6) | data formatting | bytes 9437184 | tf_op args[1]
  8.2 7.4 %all-to-all-start = ((bf16[32,1,3,4,4,1536]{5,4,2,3,1,0:T(4,128)(2,1)}), bf16[32,1,3,4,4,1536]{5,4,2,3,1,0:T(4,128)(2,1)}, u32[]{:S(2)}, u32[]{:S(2)}) async-start(bf16[32,1,3,4,4,1536]{5,4,2,3,1,0:T(4,128)(2,1)} %bitcast.128), calls=%async_computation | async-start | bytes 9437184 | tf_op jit(solution)/shard_map/all_to_all | solution.py:257
  16.4 184.4 %gather_weights.1 = (s32[32,8,128]{2,1,0:T(8,128)}, bf16[32,96,1536]{2,1,0:T(8,128)(2,1)}, bf16[32,96,1536]{2,1,0:T(8,128)(2,1)}) custom-call(s32[8,128]{1,0:T(8,128)} %pad_bitcast_fusion.code_in, bf16[96,1536]{1,0:T(8,128)(2,1)} %key_in.1, bf16[96,1536]{1,0:T(8,128)(2,1)} %value_in.1), custom_call_target="tpu_custom_call" | custom-call | flops 80000000000 | bytes 20000000 | tf_op jit(solution)/shard_map/gather_weights/pallas_call | solution.py:140
  200.8 21.8 %convolution_convert_fusion.1 = bf16[1536,1536]{0,1:T(8,128)(2,1)} fusion(bf16[1536,3072]{1,0:T(8,128)(2,1)} %bitcast.153, bf16[3072,1536]{1,0:T(8,128)(2,1)} %bitcast.156), kind=kOutput, calls=%fused_computation.1 | convolution fusion | flops 14497873920 | bytes 23592960 | tf_op jit(solution)/shard_map/dot_general | solution.py:286
  222.6 18.1 %convolution_convert_fusion = bf16[1536,1536]{0,1:T(8,128)(2,1)} fusion(bf16[1536,3072]{1,0:T(8,128)(2,1)} %bitcast.154, bf16[3072,1536]{1,0:T(8,128)(2,1)S(1)} %bitcast.155), kind=kOutput, calls=%fused_computation | convolution fusion | flops 14497873920 | bytes 23592960 | tf_op jit(solution)/shard_map/dot_general | solution.py:288
  240.7 6.5 copy.46
  247.3 8.5 %reshape.778.q_ref = bf16[4,3,128,1536]{3,2,1,0:T(8,128)(2,1)} reshape(bf16[1,4,3,32,4,1536]{5,4,3,2,1,0:T(4,128)(2,1)} %copy.46) | data formatting | bytes 9437184 | tf_op jit(solution)/shard_map/reshape | solution.py:259
  255.7 6.5 fusion.14
  269.8 35.2 %all-to-all-done.1 = bf16[32,1,1,4,4,1536]{5,4,3,2,1,0:T(4,128)(2,1)S(1)} async-done(((bf16[32,1,1,4,4,1536]{5,4,3,2,1,0:T(4,128)(2,1)}), bf16[32,1,1,4,4,1536]{5,4,3,2,1,0:T(4,128)(2,1)S(1)}, u32[]{:S(2)}, u32[]{:S(2)}) %all-to-all-start.1) | async-done | bytes 1572896 | tf_op jit(solution)/shard_map/all_to_all | solution.py:257
  308.7 3.9 reshape.783
  316.0 30.5 %all-to-all-done.2 = bf16[32,1,1,4,4,1536]{5,4,3,2,1,0:T(4,128)(2,1)S(1)} async-done(((bf16[32,1,1,4,4,1536]{5,4,3,2,1,0:T(4,128)(2,1)}), bf16[32,1,1,4,4,1536]{5,4,3,2,1,0:T(4,128)(2,1)S(1)}, u32[]{:S(2)}, u32[]{:S(2)}) %all-to-all-start.2) | async-done | bytes 1572896 | tf_op jit(solution)/shard_map/all_to_all | solution.py:257
  350.2 3.9 reshape.785
  357.6 30.4 %all-to-all-done.3 = bf16[32,1,1,4,4,1536]{5,3,4,2,1,0:T(4,128)(2,1)S(1)} async-done(((bf16[32,1,1,4,4,1536]{5,3,4,2,1,0:T(4,128)(2,1)}), bf16[32,1,1,4,4,1536]{5,3,4,2,1,0:T(4,128)(2,1)S(1)}, u32[]{:S(2)}, u32[]{:S(2)}) %all-to-all-start.3) | async-done | bytes 1572896 | tf_op jit(solution)/shard_map/all_to_all | solution.py:257
  391.7 3.9 reshape.790
  399.1 30.4 %all-to-all-done.4 = bf16[32,1,1,4,4,1536]{5,3,4,2,1,0:T(4,128)(2,1)S(1)} async-done(((bf16[32,1,1,4,4,1536]{5,3,4,2,1,0:T(4,128)(2,1)}), bf16[32,1,1,4,4,1536]{5,3,4,2,1,0:T(4,128)(2,1)S(1)}, u32[]{:S(2)}, u32[]{:S(2)}) %all-to-all-start.4) | async-done | bytes 1572896 | tf_op jit(solution)/shard_map/all_to_all | solution.py:257
  433.3 3.9 reshape.792
  440.5 30.5 %all-to-all-done.6 = bf16[32,1,1,4,4,1536]{5,3,4,2,1,0:T(4,128)(2,1)S(1)} async-done(((bf16[32,1,1,4,4,1536]{5,3,4,2,1,0:T(4,128)(2,1)}), bf16[32,1,1,4,4,1536]{5,3,4,2,1,0:T(4,128)(2,1)S(1)}, u32[]{:S(2)}, u32[]{:S(2)}) %all-to-all-start.6) | async-done | bytes 1572896 | tf_op jit(solution)/shard_map/all_to_all | solution.py:257
  478.8 14.9 %far_slot.5 = bf16[4,1,128,1664]{3,2,1,0:T(8,128)(2,1)} custom-call(bf16[4,3,128,1536]{3,2,1,0:T(8,128)(2,1)} %reshape.778.q_ref, bf16[4,3,128,1536]{3,2,1,0:T(8,128)(2,1)} %bitcast.121, bf16[4,3,128,1536]{3,2,1,0:T(8,128)(2,1)} %bitcast.125, f32[4,128,128]{2,1,0:T(8,128)} %get-tuple-element.53.bias_ref), custom_call_target="tpu_custom_call" | custom-call | flops 4026531840 | bytes 6291456 | tf_op jit(solution)/shard_map/far_slot/pallas_call | solution.py:219
  493.7 4.1 copy.76
  497.8 14.7 %all-to-all-done.7 = bf16[32,1,1,4,4,1536]{5,3,4,2,1,0:T(4,128)(2,1)S(1)} async-done(((bf16[32,1,1,4,4,1536]{5,3,4,2,1,0:T(4,128)(2,1)}), bf16[32,1,1,4,4,1536]{5,3,4,2,1,0:T(4,128)(2,1)S(1)}, u32[]{:S(2)}, u32[]{:S(2)}) %all-to-all-start.7) | async-done | bytes 1572896 | tf_op jit(solution)/shard_map/all_to_all | solution.py:257
  513.7 4.0 all-to-all-start.9
  521.0 14.9 %far_slot.3 = bf16[4,1,128,1664]{3,2,1,0:T(8,128)(2,1)} custom-call(bf16[4,3,128,1536]{3,2,1,0:T(8,128)(2,1)} %reshape.778.q_ref, bf16[4,1,128,1536]{3,2,1,0:T(8,128)(2,1)} %copy.70.k_ref, bf16[4,1,128,1536]{3,2,1,0:T(8,128)(2,1)} %copy.71.v_ref, f32[4,128,128]{2,1,0:T(8,128)} %get-tuple-element.54.bias_ref), custom_call_target="tpu_custom_call" | custom-call | flops 4026531840 | bytes 6291456 | tf_op jit(solution)/shard_map/far_slot/pallas_call | solution.py:219
  535.9 4.0 copy.72
  539.9 18.2 %all-to-all-done.9 = bf16[32,1,1,4,4,1664]{5,4,3,2,1,0:T(4,128)(2,1)S(1)} async-done(((bf16[32,1,1,4,4,1664]{5,4,3,2,1,0:T(4,128)(2,1)}), bf16[32,1,1,4,4,1664]{5,4,3,2,1,0:T(4,128)(2,1)S(1)}, u32[]{:S(2)}, u32[]{:S(2)}) %all-to-all-start.9) | async-done | bytes 1703968 | tf_op jit(solution)/shard_map/all_to_all | solution.py:257
  558.1 4.0 all-to-all-start.5
  566.6 14.9 %far_slot.4 = bf16[4,1,128,1664]{3,2,1,0:T(8,128)(2,1)} custom-call(bf16[4,3,128,1536]{3,2,1,0:T(8,128)(2,1)} %reshape.778.q_ref, bf16[4,1,128,1536]{3,2,1,0:T(8,128)(2,1)} %copy.73.k_ref, bf16[4,1,128,1536]{3,2,1,0:T(8,128)(2,1)} %copy.74.v_ref, f32[4,128,128]{2,1,0:T(8,128)} %get-tuple-element.56.bias_ref), custom_call_target="tpu_custom_call" | custom-call | flops 4026531840 | bytes 6291456 | tf_op jit(solution)/shard_map/far_slot/pallas_call | solution.py:219
  581.5 4.0 copy.75
  585.6 16.9 %all-to-all-done.5 = bf16[32,1,1,4,4,1664]{5,4,3,2,1,0:T(4,128)(2,1)S(1)} async-done(((bf16[32,1,1,4,4,1664]{5,4,3,2,1,0:T(4,128)(2,1)}), bf16[32,1,1,4,4,1664]{5,4,3,2,1,0:T(4,128)(2,1)S(1)}, u32[]{:S(2)}, u32[]{:S(2)}) %all-to-all-start.5) | async-done | bytes 1703968 | tf_op jit(solution)/shard_map/all_to_all | solution.py:257
  602.5 4.3 all-to-all-start.8
  626.0 20.4 %near_slot.3.rest_0_ = bf16[4,3,128,1536]{3,2,1,0:T(8,128)(2,1)} custom-call(bf16[4,3,128,1536]{3,2,1,0:T(8,128)(2,1)} %bitcast.117, bf16[4,3,128,1536]{3,2,1,0:T(8,128)(2,1)} %bitcast.122, bf16[4,3,128,1536]{3,2,1,0:T(8,128)(2,1)} %bitcast.126, f32[4,128,128]{2,1,0:T(8,128)} %get-tuple-element.57.bias_ref, bf16[4,1,128,1664]{3,2,1,0:T(8,128)(2,1)} %reshape.797.back_ref), custom_call_target="tpu_custom_call" | custom-call | flops 4026531840 | bytes 6291456 | tf_op jit(solution)/shard_map/near_slot/pallas_call | solution.py:241
  652.0 20.4 %near_slot.4.rest_0_ = bf16[4,3,128,1536]{3,2,1,0:T(8,128)(2,1)} custom-call(bf16[4,3,128,1536]{3,2,1,0:T(8,128)(2,1)} %bitcast.118, bf16[4,3,128,1536]{3,2,1,0:T(8,128)(2,1)} %bitcast.123, bf16[4,3,128,1536]{3,2,1,0:T(8,128)(2,1)} %bitcast.127, f32[4,128,128]{2,1,0:T(8,128)} %get-tuple-element.55.bias_ref, ...), custom_call_target="tpu_custom_call", output_to_operand_aliasing={{}: (5, {})} | custom-call | flops 4026531840 | bytes 6291456 | tf_op jit(solution)/shard_map/near_slot/pallas_call | solution.py:241
  672.5 20.4 %near_slot.5 = bf16[4,3,128,1536]{3,2,1,0:T(8,128)(2,1)} custom-call(bf16[4,3,128,1536]{3,2,1,0:T(8,128)(2,1)} %bitcast.119, bf16[4,1,128,1536]{3,2,1,0:T(8,128)(2,1)} %reshape.780.k_ref, bf16[4,1,128,1536]{3,2,1,0:T(8,128)(2,1)} %reshape.782.v_ref, f32[4,128,128]{2,1,0:T(8,128)} %get-tuple-element.58.bias_ref, ...), custom_call_target="tpu_custom_call", output_to_operand_aliasing={{}: (5, {})} | custom-call | flops 4026531840 | bytes 6291456 | tf_op jit(solution)/shard_map/near_slot/pallas_call | solution.py:241
  (75 shorter events, 78.6 us)
Async XLA Ops:
  8.2 7.4 %copy-start.10 = (s32[1,4,3,2,2]{1,4,3,2,0:T(2,128)S(1)}, s32[1,4,3,2,2]{1,4,3,2,0:T(2,128)}, u32[]{:S(2)}) copy-start(s32[1,4,3,2,2]{1,4,3,2,0:T(2,128)} %param.9) | copy-start | bytes 580
  8.2 232.6 %all-to-all-start = ((bf16[32,1,3,4,4,1536]{5,4,2,3,1,0:T(4,128)(2,1)}), bf16[32,1,3,4,4,1536]{5,4,2,3,1,0:T(4,128)(2,1)}, u32[]{:S(2)}, u32[]{:S(2)}) async-start(bf16[32,1,3,4,4,1536]{5,4,2,3,1,0:T(4,128)(2,1)} %bitcast.128), calls=%async_computation | async-start | bytes 9437184 | tf_op jit(solution)/shard_map/all_to_all | solution.py:257
  200.8 21.8 %copy-start.12 = (bf16[32,96,1536]{2,1,0:T(8,128)(2,1)S(1)}, bf16[32,96,1536]{2,1,0:T(8,128)(2,1)}, u32[]{:S(2)}) copy-start(bf16[32,96,1536]{2,1,0:T(8,128)(2,1)} %get-tuple-element.12) | copy-start | bytes 28311556
  264.6 40.4 %all-to-all-start.1 = ((bf16[32,1,1,4,4,1536]{5,4,3,2,1,0:T(4,128)(2,1)}), bf16[32,1,1,4,4,1536]{5,4,3,2,1,0:T(4,128)(2,1)S(1)}, u32[]{:S(2)}, u32[]{:S(2)}) async-start(bf16[32,1,1,4,4,1536]{5,4,3,2,1,0:T(4,128)(2,1)} %bitcast.144), calls=%async_computation.1 | async-start | bytes 3145728 | tf_op jit(solution)/shard_map/all_to_all | solution.py:257
  305.0 7.6 %copy-start = (bf16[32,1,1,4,4,1536]{5,4,3,2,1,0:T(4,128)(2,1)}, bf16[32,1,1,4,4,1536]{5,4,3,2,1,0:T(4,128)(2,1)S(1)}, u32[]{:S(2)}) copy-start(bf16[32,1,1,4,4,1536]{5,4,3,2,1,0:T(4,128)(2,1)S(1)} %all-to-all-done.1) | copy-start | bytes 4718596
  305.0 41.5 %all-to-all-start.2 = ((bf16[32,1,1,4,4,1536]{5,4,3,2,1,0:T(4,128)(2,1)}), bf16[32,1,1,4,4,1536]{5,4,3,2,1,0:T(4,128)(2,1)S(1)}, u32[]{:S(2)}, u32[]{:S(2)}) async-start(bf16[32,1,1,4,4,1536]{5,4,3,2,1,0:T(4,128)(2,1)} %bitcast.141), calls=%async_computation.2 | async-start | bytes 3145728 | tf_op jit(solution)/shard_map/all_to_all | solution.py:257
  346.4 7.6 %copy-start.1 = (bf16[32,1,1,4,4,1536]{5,4,3,2,1,0:T(4,128)(2,1)}, bf16[32,1,1,4,4,1536]{5,4,3,2,1,0:T(4,128)(2,1)S(1)}, u32[]{:S(2)}) copy-start(bf16[32,1,1,4,4,1536]{5,4,3,2,1,0:T(4,128)(2,1)S(1)} %all-to-all-done.2) | copy-start | bytes 4718596
  346.4 41.5 %all-to-all-start.3 = ((bf16[32,1,1,4,4,1536]{5,3,4,2,1,0:T(4,128)(2,1)}), bf16[32,1,1,4,4,1536]{5,3,4,2,1,0:T(4,128)(2,1)S(1)}, u32[]{:S(2)}, u32[]{:S(2)}) async-start(bf16[32,1,1,4,4,1536]{5,3,4,2,1,0:T(4,128)(2,1)} %bitcast.142), calls=%async_computation.3 | async-start | bytes 3145728 | tf_op jit(solution)/shard_map/all_to_all | solution.py:257
  388.0 7.7 %copy-start.2 = (bf16[32,1,1,4,4,1536]{5,3,4,2,1,0:T(4,128)(2,1)}, bf16[32,1,1,4,4,1536]{5,3,4,2,1,0:T(4,128)(2,1)S(1)}, u32[]{:S(2)}) copy-start(bf16[32,1,1,4,4,1536]{5,3,4,2,1,0:T(4,128)(2,1)S(1)} %all-to-all-done.3) | copy-start | bytes 4718596
  388.0 41.5 %all-to-all-start.4 = ((bf16[32,1,1,4,4,1536]{5,3,4,2,1,0:T(4,128)(2,1)}), bf16[32,1,1,4,4,1536]{5,3,4,2,1,0:T(4,128)(2,1)S(1)}, u32[]{:S(2)}, u32[]{:S(2)}) async-start(bf16[32,1,1,4,4,1536]{5,3,4,2,1,0:T(4,128)(2,1)} %bitcast.143), calls=%async_computation.4 | async-start | bytes 3145728 | tf_op jit(solution)/shard_map/all_to_all | solution.py:257
  429.5 7.7 %copy-start.5 = (bf16[32,1,1,4,4,1536]{5,3,4,2,1,0:T(4,128)(2,1)}, bf16[32,1,1,4,4,1536]{5,3,4,2,1,0:T(4,128)(2,1)S(1)}, u32[]{:S(2)}) copy-start(bf16[32,1,1,4,4,1536]{5,3,4,2,1,0:T(4,128)(2,1)S(1)} %all-to-all-done.4) | copy-start | bytes 4718596
  429.5 41.5 %all-to-all-start.6 = ((bf16[32,1,1,4,4,1536]{5,3,4,2,1,0:T(4,128)(2,1)}), bf16[32,1,1,4,4,1536]{5,3,4,2,1,0:T(4,128)(2,1)S(1)}, u32[]{:S(2)}, u32[]{:S(2)}) async-start(bf16[32,1,1,4,4,1536]{5,3,4,2,1,0:T(4,128)(2,1)} %bitcast.140), calls=%async_computation.6 | async-start | bytes 3145728 | tf_op jit(solution)/shard_map/all_to_all | solution.py:257
  440.5 34.3 %copy-start.9 = (s32[32,8,128]{2,1,0:T(8,128)S(1)}, s32[32,8,128]{2,1,0:T(8,128)}, u32[]{:S(2)}) copy-start(s32[32,8,128]{2,1,0:T(8,128)} %get-tuple-element.16) | copy-start | bytes 393220
  471.0 3.8 copy-start.4
  471.0 41.5 %all-to-all-start.7 = ((bf16[32,1,1,4,4,1536]{5,3,4,2,1,0:T(4,128)(2,1)}), bf16[32,1,1,4,4,1536]{5,3,4,2,1,0:T(4,128)(2,1)S(1)}, u32[]{:S(2)}, u32[]{:S(2)}) async-start(bf16[32,1,1,4,4,1536]{5,3,4,2,1,0:T(4,128)(2,1)} %bitcast.139), calls=%async_computation.7 | async-start | bytes 3145728 | tf_op jit(solution)/shard_map/all_to_all | solution.py:257
  474.8 1.4 copy-start.11
  512.5 1.2 copy-start.7
  513.7 4.0 copy-start.3
  513.7 44.4 %all-to-all-start.9 = ((bf16[32,1,1,4,4,1664]{5,4,3,2,1,0:T(4,128)(2,1)}), bf16[32,1,1,4,4,1664]{5,4,3,2,1,0:T(4,128)(2,1)S(1)}, u32[]{:S(2)}, u32[]{:S(2)}) async-start(bf16[32,1,1,4,4,1664]{5,4,3,2,1,0:T(4,128)(2,1)} %bitcast.55), calls=%async_computation.9 | async-start | bytes 3407872 | tf_op jit(solution)/shard_map/all_to_all | solution.py:257
  517.7 1.8 copy-start.6
  558.1 44.4 %all-to-all-start.5 = ((bf16[32,1,1,4,4,1664]{5,4,3,2,1,0:T(4,128)(2,1)}), bf16[32,1,1,4,4,1664]{5,4,3,2,1,0:T(4,128)(2,1)S(1)}, u32[]{:S(2)}, u32[]{:S(2)}) async-start(bf16[32,1,1,4,4,1664]{5,4,3,2,1,0:T(4,128)(2,1)} %bitcast.132), calls=%async_computation.5 | async-start | bytes 3407872 | tf_op jit(solution)/shard_map/all_to_all | solution.py:257
  562.1 3.0 copy-start.8
  602.5 46.0 %all-to-all-start.8 = ((bf16[32,1,1,4,4,1664]{5,4,3,2,1,0:T(4,128)(2,1)}), bf16[32,1,1,4,4,1664]{5,4,3,2,1,0:T(4,128)(2,1)}, u32[]{:S(2)}, u32[]{:S(2)}) async-start(bf16[32,1,1,4,4,1664]{5,4,3,2,1,0:T(4,128)(2,1)} %bitcast.131), calls=%async_computation.8 | async-start | bytes 3407872 | tf_op jit(solution)/shard_map/all_to_all | solution.py:257

commit v2 on v1

--- a/solution.py
+++ b/solution.py
@@ -180,22 +180,41 @@
     stats = jnp.zeros(lane.shape, jnp.float32)
     for head in range(heads):
         partial, peak, total = one_slot(q_ref, k_ref, v_ref, bias, head)
-        out_ref[0, 0, :, pl.ds(head * HDIM, HDIM)] = (partial / total).astype(jnp.bfloat16)
+        out_ref[0, 0, :, pl.ds(head * HDIM, HDIM)] = (partial / total).astype(out_ref.dtype)
         for at, part in enumerate(three_parts(peak) + three_parts(total)):
-            stats = jnp.where(lane == 6 * head + at, part, stats)
-    out_ref[0, 0, :, pl.ds(heads * HDIM, LANES)] = stats.astype(jnp.bfloat16)
+            stats = jnp.where(lane == at * heads + head, part, stats)
+    out_ref[0, 0, :, pl.ds(heads * HDIM, LANES)] = stats.astype(out_ref.dtype)
+
+
+def read_stats(ref, heads):
+    stats = ref[0, 0, :, pl.ds(heads * HDIM, LANES)].astype(jnp.float32)
+    parts = [stats[:, at * heads : (at + 1) * heads] for at in range(6)]
+    return parts[0] + parts[1] + parts[2], parts[3] + parts[4] + parts[5]
+
+
+def merge_kernel(heads, near_ref, back_ref, so_far_ref, out_ref):
+    near_peak, near_total = read_stats(near_ref, heads)
+    far_peak, far_total = read_stats(back_ref, heads)
+    top = jnp.maximum(near_peak, far_peak)
+    near_w = near_total * jnp.exp(near_peak - top)
+    far_w = far_total * jnp.exp(far_peak - top)
+    scale = 1.0 / (near_w + far_w)
+    near_w, far_w = near_w * scale, far_w * scale
+    for head in range(heads):
+        cols = pl.ds(head * HDIM, HDIM)
+        mixed = near_ref[0, 0, :, cols] * near_w[:, head : head + 1]
+        mixed += back_ref[0, 0, :, cols].astype(jnp.float32) * far_w[:, head : head + 1]
+        out_ref[0, 0, :, cols] = mixed.astype(jnp.bfloat16)
 
 
 def near_kernel(heads, q_ref, k_ref, v_ref, bias_ref, back_ref, *rest):
     out_ref = rest[-1]
     bias = bias_ref[0]
-    stats = back_ref[0, 0, :, pl.ds(heads * HDIM, LANES)].astype(jnp.float32)
+    far_peaks, far_totals = read_stats(back_ref, heads)
     for head in range(heads):
         cols = pl.ds(head * HDIM, HDIM)
         partial, peak, total = one_slot(q_ref, k_ref, v_ref, bias, head)
-        col = [stats[:, 6 * head + at : 6 * head + at + 1] for at in range(6)]
-        far_peak = col[0] + col[1] + col[2]
-        far_total = col[3] + col[4] + col[5]
+        far_peak, far_total = far_peaks[:, head : head + 1], far_totals[:, head : head + 1]
         top = jnp.maximum(peak, far_peak)
         near_w = jnp.exp(peak - top)
         far_w = jnp.exp(far_peak - top) * far_total
@@ -209,11 +228,11 @@
 
 def attend_cost(groups, rows, keys, width):
     return pl.CostEstimate(
-        flops=40 * groups * rows * keys * width, bytes_accessed=8 * groups * rows * width, transcendentals=0
+        flops=150 * groups * rows * keys * width, bytes_accessed=8 * groups * rows * width, transcendentals=0
     )
 
 
-def far_part(operands, bias):
+def far_part(operands, bias, kind=jnp.bfloat16):
     groups, rows, keys = bias.shape
     width = operands[0][0].shape[-1]
     return pl.pallas_call(
@@ -221,17 +240,17 @@
         grid=(groups,),
         in_specs=[plane_spec(a, p) for a, p in operands] + [pl.BlockSpec((1, rows, keys), lambda g: (g, 0, 0))],
         out_specs=pl.BlockSpec((1, 1, rows, width + LANES), lambda g: (g, 0, 0, 0)),
-        out_shape=jax.ShapeDtypeStruct((groups, 1, rows, width + LANES), jnp.bfloat16),
+        out_shape=jax.ShapeDtypeStruct((groups, 1, rows, width + LANES), kind),
         cost_estimate=attend_cost(groups, rows, keys, width),
         name="far_slot",
     )(*[a for a, _ in operands], bias)
 
 
-def near_part(operands, bias, back, plane, planes, so_far):
+def near_part(operands, bias, back, back_plane, plane, planes, so_far):
     groups, rows, keys = bias.shape
     width = operands[0][0].shape[-1]
     in_specs = [plane_spec(a, p) for a, p in operands]
-    in_specs += [pl.BlockSpec((1, rows, keys), lambda g: (g, 0, 0)), plane_spec(back, 0)]
+    in_specs += [pl.BlockSpec((1, rows, keys), lambda g: (g, 0, 0)), plane_spec(back, back_plane)]
     args = [a for a, _ in operands] + [bias, back]
     aliases = {}
     if so_far is not None:
@@ -250,13 +269,28 @@
     )(*args)
 
 
-def swap_lines(array, scenes, size):
+def merge_part(near, back, plane, so_far):
+    groups, planes, rows, width = so_far.shape
+    return pl.pallas_call(
+        functools.partial(merge_kernel, width // HDIM),
+        grid=(groups,),
+        in_specs=[plane_spec(near, 0), plane_spec(back, 0), pl.BlockSpec(memory_space=pl.ANY)],
+        out_specs=pl.BlockSpec((1, 1, rows, width), lambda g: (g, plane, 0, 0)),
+        out_shape=jax.ShapeDtypeStruct(so_far.shape, so_far.dtype),
+        input_output_aliases={2: 0},
+        name="merge_slots",
+    )(near, back, so_far)
+
+
+def cut_lines(array, scenes, size):
     groups, planes, positions, width = array.shape
     lines, own = groups // scenes, positions // size
-    cut = array.reshape(scenes, lines, planes, size, own, width).transpose(3, 0, 2, 4, 1, 5)
+    return array.reshape(scenes, lines, planes, size, own, width).transpose(3, 0, 2, 4, 1, 5)
+
+
+def swap_cut(cut):
     got = lax.all_to_all(cut, "seq", split_axis=0, concat_axis=0, tiled=True)
-    got = got.transpose(1, 3, 2, 0, 4, 5)
-    return got.reshape(scenes * own, planes, size * lines, width)
+    return got, got.transpose(1, 3, 2, 0, 4, 5)
 
 
 def keep_bias(codes, keys):
@@ -270,7 +304,14 @@
     width = queries.shape[-1]
     groups = scenes * lines
     q_home = queries.reshape(groups, planes, positions, width)
-    swap = functools.partial(swap_lines, scenes=scenes, size=size)
+
+    def cut(*arrays):
+        return jnp.concatenate([cut_lines(a, scenes, size) for a in arrays], axis=2)
+
+    def swap(blocks, *after):
+        blocks = lax.optimization_barrier((blocks,) + after)[0]
+        got, turned = swap_cut(blocks)
+        return got, turned.reshape(-1, turned.shape[2], size * turned.shape[4], turned.shape[5])
 
     flat_codes = halves.reshape(-1)
     padded = -(-flat_codes.size // (8 * LANES)) * 8 * LANES
@@ -279,7 +320,8 @@
     code_all = code_all.reshape(size, -1)[:, : flat_codes.size].reshape((size,) + halves.shape)
     code_all = jnp.moveaxis(code_all, 0, 1).reshape(scenes, size * lines, planes, 2, 2)
 
-    q_moved = swap(q_home)
+    q0_got, q0 = swap(cut(q_home[:, :1]))
+    q12_got, q12 = swap(cut(q_home[:, 1:]), key_all)
 
     home_rows = tokens.reshape(-1, depth)
     home_shape = (groups, planes, positions, width)
@@ -288,11 +330,6 @@
     values = jnp.dot(home_rows, value_all.reshape(depth, width), preferred_element_type=jnp.float32)
     values = values.astype(jnp.bfloat16).reshape(home_shape)
 
-    keys, values, q_moved = lax.optimization_barrier((keys, values, q_moved))
-    k2, v2 = swap(keys[:, 2:]), swap(values[:, 2:])
-    k1, v1 = swap(keys[:, 1:2]), swap(values[:, 1:2])
-    k0, v0 = swap(keys[:, :1]), swap(values[:, :1])
-
     own = positions // size
     own_half = (lax.axis_index("seq") * own + jnp.arange(own)) // (positions // 2)
     home_half = jnp.arange(positions) // (positions // 2)
@@ -307,16 +344,19 @@
         codes = jnp.where(home_half[None, :] == 0, pairs[..., 0], pairs[..., 1])
         return keep_bias(codes, positions)
 
-    def back(far):
-        return swap_lines(far, scenes, size)
-
-    back0 = back(far_part(((q_moved, 0), (keys, 2), (values, 2)), far_bias(0)))
-    back1 = back(far_part(((q_moved, 1), (k2, 0), (v2, 0)), far_bias(1)))
-    back2 = back(far_part(((q_moved, 2), (k1, 0), (v1, 0)), far_bias(2)))
-
-    out = near_part(((q_home, 0), (keys, 1), (values, 1)), near_bias(0), back0, 0, planes, None)
-    out = near_part(((q_home, 1), (keys, 0), (values, 0)), near_bias(1), back1, 1, planes, out)
-    out = near_part(((q_home, 2), (k0, 0), (v0, 0)), near_bias(2), back2, 2, planes, out)
+    kv2_got, kv2 = swap(cut(keys[:, 2:], values[:, 2:]), q0_got, q12_got)
+    kv1_got, kv1 = swap(cut(keys[:, 1:2], values[:, 1:2]), kv2_got)
+    far0 = far_part(((q0, 0), (keys, 2), (values, 2)), far_bias(0))
+    far1 = far_part(((q12, 0), (kv2, 0), (kv2, 1)), far_bias(1))
+    back01_got, back01 = swap(cut(far0, far1), kv1_got)
+    kv0_got, kv0 = swap(cut(keys[:, :1], values[:, :1]), back01_got)
+    far2 = far_part(((q12, 1), (kv1, 0), (kv1, 1)), far_bias(2))
+    _, back2 = swap(cut(far2), kv0_got)
+
+    out = near_part(((q_home, 0), (keys, 1), (values, 1)), near_bias(0), back01, 0, 0, planes, None)
+    out = near_part(((q_home, 1), (keys, 0), (values, 0)), near_bias(1), back01, 1, 1, planes, out)
+    near2 = far_part(((q_home, 2), (kv0, 0), (kv0, 1)), near_bias(2), jnp.float32)
+    out = merge_part(near2, back2, 2, out)
     return out.reshape(queries.shape)
 
 

time: 700 us -> 604 us (0.86)
  Pallas kernels: 290 us -> 223 us
  waiting for transfers between devices: 207 us -> 171 us
  other arithmetic: 2.59 us -> 17.5 us
  starting transfers between devices: 41.2 us -> 31.8 us
    pallas_call x1, Pallas kernels: 184 us -> 117 us  [gather_all(): pl.pallas_call(functools.partial(gather_kernel, side, side), out_shape=[j...]
    all_to_all x10 -> x7, waiting for transfers between devices: 207 us -> 171 us  [swap_cut(): got = lax.all_to_all(cut, 'seq', split_axis=0, concat_axis=0, tiled=True)]
    pallas_call x3 -> x2, Pallas kernels: 61.3 us -> 40.5 us  [near_part(): pl.pallas_call(functools.partial(near_kernel, width // HDIM), grid=(group...]
    pallas_call x3 -> x4, Pallas kernels: 44.7 us -> 59.9 us  [far_part(): pl.pallas_call(functools.partial(far_kernel, width // HDIM), grid=(groups...]
    concatenate x0 -> x4, other arithmetic: none -> 14.9 us  [cut(): return jnp.concatenate([cut_lines(a, scenes, size) for a in arrays], axis=2)]
    transpose x6 -> x8, local copies, waits for them, and re-layouts: 17.1 us -> 27 us  [the longest x5 16.1 us: swap_cut(): return (got, got.transpose(1, 3, 2, 0, 4, 5))]
    all_to_all x10 -> x7, starting transfers between devices: 41.2 us -> 31.8 us  [swap_cut(): got = lax.all_to_all(cut, 'seq', split_axis=0, concat_axis=0, tiled=True)]
    unnamed x29 -> x12, local copies, waits for them, and re-layouts: 9.93 us -> 2.71 us
  transfers between devices with their start and end apart: 10 -> 7, of which waited for: 8 -> 5; matrix products, arithmetic and copies ran while one was open for 17% -> 27% of each run, Pallas kernels for 36% -> 36%
where the time goes in v2:
time: 604 us; the launch traced here: 598 us
  Pallas kernels  223 us (37%)
  waiting for transfers between devices  171 us (28%)
  local copies, waits for them, and re-layouts  115 us (19%)
  matrix products  39.9 us (7%)
  starting transfers between devices  31.8 us (5%)
  other arithmetic  17.5 us (3%)
    all_to_all x7, waiting for transfers between devices, swap_cut(): got = lax.all_to_all(cut, 'seq', split_axis=0, concat_axis=0, tiled=True)  171 us
    pallas_call x1, Pallas kernels, gather_all(): pl.pallas_call(functools.partial(gather_kernel, side, side), out_shape=[j...  117 us
    pallas_call x4, Pallas kernels, far_part(): pl.pallas_call(functools.partial(far_kernel, width // HDIM), grid=(groups...  59.9 us
    reshape x13, local copies, waits for them, and re-layouts, cut_lines(): array.reshape(scenes, lines, planes, size, own, width)  44.8 us
    pallas_call x2, Pallas kernels, near_part(): pl.pallas_call(functools.partial(near_kernel, width // HDIM), grid=(group...  40.5 us
    all_to_all x7, starting transfers between devices, swap_cut(): got = lax.all_to_all(cut, 'seq', split_axis=0, concat_axis=0, tiled=True)  31.8 us
    reshape x7, local copies, waits for them, and re-layouts, swap(): turned.reshape(-1, turned.shape[2], size * turned.shape[4], turned.shape[5])  24.2 us
    dot_general x1, matrix products, on_device(): jnp.dot(home_rows, key_all.reshape(depth, width), preferred_element_type=...  19.9 us
  transfers between devices with their start and end apart: 7, of which 5 were waited for; matrix products, arithmetic and copies ran while one was open for 27% of the time, Pallas kernels for 36%

profile of v2, /device:TPU:0, one launch (start us, length us, event | category | flops | bytes accessed | tf_op | source)
XLA Modules:
  0.0 598.4 jit_solution(3000373801436495599)
XLA Ops:
  3.9 7.4 %all-to-all-start = ((bf16[32,1,1,4,4,1536]{5,3,4,2,1,0:T(4,128)(2,1)}), bf16[32,1,1,4,4,1536]{5,3,4,2,1,0:T(4,128)(2,1)}, u32[]{:S(2)}, u32[]{:S(2)}) async-start(bf16[32,1,1,4,4,1536]{5,3,4,2,1,0:T(4,128)(2,1)} %bitcast.105), calls=%async_computation | async-start | bytes 3145728 | tf_op jit(solution)/shard_map/all_to_all | solution.py:292
  12.2 116.8 %gather_weights.1 = (s32[32,8,128]{2,1,0:T(8,128)}, bf16[32,96,1536]{2,1,0:T(8,128)(2,1)}, bf16[32,96,1536]{2,1,0:T(8,128)(2,1)}) custom-call(s32[8,128]{1,0:T(8,128)} %pad_bitcast_fusion.code_in, bf16[96,1536]{1,0:T(8,128)(2,1)} %key_in.1, bf16[96,1536]{1,0:T(8,128)(2,1)} %value_in.1), custom_call_target="tpu_custom_call" | custom-call | flops 80000000000 | bytes 20000000 | tf_op jit(solution)/shard_map/gather_weights/pallas_call | solution.py:140
  132.7 4.8 reshape.781
  144.2 19.9 %convolution_convert_fusion.1 = bf16[1536,1536]{0,1:T(8,128)(2,1)S(1)} fusion(bf16[1536,3072]{1,0:T(8,128)(2,1)} %bitcast.133, bf16[3072,1536]{1,0:T(8,128)(2,1)} %bitcast.136), kind=kOutput, calls=%fused_computation.1 | convolution fusion | flops 14497873920 | bytes 23592960 | tf_op jit(solution)/shard_map/dot_general | solution.py:328
  167.8 3.8 reshape.783
  171.6 19.9 %convolution_convert_fusion = bf16[1536,1536]{0,1:T(8,128)(2,1)S(1)} fusion(bf16[1536,3072]{1,0:T(8,128)(2,1)} %bitcast.134, bf16[3072,1536]{1,0:T(8,128)(2,1)} %bitcast.135), kind=kOutput, calls=%fused_computation | convolution fusion | flops 14497873920 | bytes 23592960 | tf_op jit(solution)/shard_map/dot_general | solution.py:330
  195.4 4.0 reshape.784
  206.7 8.9 %all-to-all-done.1 = bf16[32,1,2,4,4,1536]{5,3,2,4,1,0:T(4,128)(2,1)S(1)} async-done(((bf16[32,1,2,4,4,1536]{5,3,2,4,1,0:T(4,128)(2,1)}), bf16[32,1,2,4,4,1536]{5,3,2,4,1,0:T(4,128)(2,1)S(1)}, u32[]{:S(2)}, u32[]{:S(2)}) %all-to-all-start.1) | async-done | bytes 3145760 | tf_op jit(solution)/shard_map/all_to_all | solution.py:292
  215.6 4.1 all-to-all-start.2
  219.7 3.9 reshape.787
  234.7 56.4 %all-to-all-done.2 = bf16[32,1,2,4,4,1536]{5,3,4,2,1,0:T(4,128)(2,1)} async-done(((bf16[32,1,2,4,4,1536]{5,3,4,2,1,0:T(4,128)(2,1)}), bf16[32,1,2,4,4,1536]{5,3,4,2,1,0:T(4,128)(2,1)}, u32[]{:S(2)}, u32[]{:S(2)}) %all-to-all-start.2) | async-done | bytes 3145760 | tf_op jit(solution)/shard_map/all_to_all | solution.py:292
  291.1 4.3 all-to-all-start.3
  306.3 14.9 %far_slot.4 = bf16[4,1,128,1664]{3,2,1,0:T(8,128)(2,1)} custom-call(bf16[4,1,128,1536]{3,2,1,0:T(8,128)(2,1)} %copy.60.q_ref, bf16[4,3,128,1536]{3,2,1,0:T(8,128)(2,1)} %bitcast.118, bf16[4,3,128,1536]{3,2,1,0:T(8,128)(2,1)} %bitcast.122, f32[4,128,128]{2,1,0:T(8,128)} %get-tuple-element.64.bias_ref), custom_call_target="tpu_custom_call" | custom-call | flops 15099494400 | bytes 6291456 | tf_op jit(solution)/shard_map/far_slot/pallas_call | solution.py:238
  321.2 4.1 copy.61
  333.4 15.1 %far_slot.5 = bf16[4,1,128,1664]{3,2,1,0:T(8,128)(2,1)} custom-call(bf16[4,2,128,1536]{3,2,1,0:T(8,128)(2,1)} %copy.62.q_ref, bf16[4,2,128,1536]{3,2,1,0:T(8,128)(2,1)} %reshape.785.k_ref.v_ref, bf16[4,2,128,1536]{3,2,1,0:T(8,128)(2,1)} %reshape.785.k_ref.v_ref, f32[4,128,128]{2,1,0:T(8,128)} %get-tuple-element.60.bias_ref), custom_call_target="tpu_custom_call" | custom-call | flops 15099494400 | bytes 6291456 | tf_op jit(solution)/shard_map/far_slot/pallas_call | solution.py:238
  351.4 4.0 pad_maximum_fusion
  355.4 11.4 %all-to-all-done.3 = bf16[32,1,2,4,4,1536]{5,3,4,2,1,0:T(4,128)(2,1)} async-done(((bf16[32,1,2,4,4,1536]{5,3,4,2,1,0:T(4,128)(2,1)}), bf16[32,1,2,4,4,1536]{5,3,4,2,1,0:T(4,128)(2,1)}, u32[]{:S(2)}, u32[]{:S(2)}) %all-to-all-start.3) | async-done | bytes 3145760 | tf_op jit(solution)/shard_map/all_to_all | solution.py:292
  366.8 3.9 all-to-all-start.4
  370.8 3.9 reshape.773
  385.8 62.0 %all-to-all-done.4 = bf16[32,1,2,4,4,1664]{5,4,2,3,1,0:T(4,128)(2,1)S(1)} async-done(((bf16[32,1,2,4,4,1664]{5,4,2,3,1,0:T(4,128)(2,1)}), bf16[32,1,2,4,4,1664]{5,4,2,3,1,0:T(4,128)(2,1)S(1)}, u32[]{:S(2)}, u32[]{:S(2)}) %all-to-all-start.4) | async-done | bytes 3407904 | tf_op jit(solution)/shard_map/all_to_all | solution.py:292
  447.8 4.5 all-to-all-start.5
  452.4 4.8 copy.55
  457.1 5.9 reshape.790.k_ref.v_ref
  463.1 14.9 %far_slot.7 = bf16[4,1,128,1664]{3,2,1,0:T(8,128)(2,1)} custom-call(bf16[4,2,128,1536]{3,2,1,0:T(8,128)(2,1)} %copy.62.q_ref, bf16[4,2,128,1536]{3,2,1,0:T(8,128)(2,1)} %reshape.790.k_ref.v_ref, bf16[4,2,128,1536]{3,2,1,0:T(8,128)(2,1)} %reshape.790.k_ref.v_ref, f32[4,128,128]{2,1,0:T(8,128)} %get-tuple-element.62.bias_ref), custom_call_target="tpu_custom_call" | custom-call | flops 15099494400 | bytes 6291456 | tf_op jit(solution)/shard_map/far_slot/pallas_call | solution.py:238
  478.0 4.0 copy.64
  485.0 6.6 %reshape.793.back_ref = bf16[4,2,128,1664]{3,2,1,0:T(8,128)(2,1)} reshape(bf16[1,4,2,32,4,1664]{5,4,3,2,1,0:T(4,128)(2,1)} %copy.59) | data formatting | bytes 6815744 | tf_op jit(solution)/shard_map/reshape | solution.py:314
  491.6 32.2 %all-to-all-done.5 = bf16[32,1,2,4,4,1536]{5,3,4,2,1,0:T(4,128)(2,1)} async-done(((bf16[32,1,2,4,4,1536]{5,3,4,2,1,0:T(4,128)(2,1)}), bf16[32,1,2,4,4,1536]{5,3,4,2,1,0:T(4,128)(2,1)}, u32[]{:S(2)}, u32[]{:S(2)}) %all-to-all-start.5) | async-done | bytes 3145760 | tf_op jit(solution)/shard_map/all_to_all | solution.py:292
  523.8 4.2 all-to-all-start.6
  528.0 20.2 %near_slot.2.rest_0_ = bf16[4,3,128,1536]{3,2,1,0:T(8,128)(2,1)} custom-call(bf16[4,3,128,1536]{3,2,1,0:T(8,128)(2,1)} %bitcast.114, bf16[4,3,128,1536]{3,2,1,0:T(8,128)(2,1)} %bitcast.119, bf16[4,3,128,1536]{3,2,1,0:T(8,128)(2,1)} %bitcast.123, f32[4,128,128]{2,1,0:T(8,128)} %get-tuple-element.59.bias_ref, bf16[4,2,128,1664]{3,2,1,0:T(8,128)(2,1)} %reshape.793.back_ref), custom_call_target="tpu_custom_call" | custom-call | flops 15099494400 | bytes 6291456 | tf_op jit(solution)/shard_map/near_slot/pallas_call | solution.py:260
  548.3 20.2 %near_slot.3.so_far_ref = bf16[4,3,128,1536]{3,2,1,0:T(8,128)(2,1)} custom-call(bf16[4,3,128,1536]{3,2,1,0:T(8,128)(2,1)} %bitcast.115, bf16[4,3,128,1536]{3,2,1,0:T(8,128)(2,1)} %bitcast.120, bf16[4,3,128,1536]{3,2,1,0:T(8,128)(2,1)} %bitcast.124, f32[4,128,128]{2,1,0:T(8,128)} %get-tuple-element.63.bias_ref, ...), custom_call_target="tpu_custom_call", output_to_operand_aliasing={{}: (5, {})} | custom-call | flops 15099494400 | bytes 6291456 | tf_op jit(solution)/shard_map/near_slot/pallas_call | solution.py:260
  574.0 15.0 %far_slot.6.near_ref = f32[4,1,128,1664]{3,2,1,0:T(8,128)} custom-call(bf16[4,3,128,1536]{3,2,1,0:T(8,128)(2,1)} %bitcast.116, bf16[4,2,128,1536]{3,2,1,0:T(8,128)(2,1)} %reshape.789.k_ref.v_ref, bf16[4,2,128,1536]{3,2,1,0:T(8,128)(2,1)} %reshape.789.k_ref.v_ref, f32[4,128,128]{2,1,0:T(8,128)} %get-tuple-element.61.bias_ref), custom_call_target="tpu_custom_call" | custom-call | flops 15099494400 | bytes 6291456 | tf_op jit(solution)/shard_map/far_slot/pallas_call | solution.py:238
  592.5 5.7 merge_slots.1
  (59 shorter events, 86.0 us)
Async XLA Ops:
  1.9 9.4 %copy-start.4 = (s32[1,4,3,2,2]{1,4,3,2,0:T(2,128)S(1)}, s32[1,4,3,2,2]{1,4,3,2,0:T(2,128)}, u32[]{:S(2)}) copy-start(s32[1,4,3,2,2]{1,4,3,2,0:T(2,128)} %param.9) | copy-start | bytes 580
  3.9 137.0 %all-to-all-start = ((bf16[32,1,1,4,4,1536]{5,3,4,2,1,0:T(4,128)(2,1)}), bf16[32,1,1,4,4,1536]{5,3,4,2,1,0:T(4,128)(2,1)}, u32[]{:S(2)}, u32[]{:S(2)}) async-start(bf16[32,1,1,4,4,1536]{5,3,4,2,1,0:T(4,128)(2,1)} %bitcast.105), calls=%async_computation | async-start | bytes 3145728 | tf_op jit(solution)/shard_map/all_to_all | solution.py:292
  140.9 74.7 %all-to-all-start.1 = ((bf16[32,1,2,4,4,1536]{5,3,2,4,1,0:T(4,128)(2,1)}), bf16[32,1,2,4,4,1536]{5,3,2,4,1,0:T(4,128)(2,1)S(1)}, u32[]{:S(2)}, u32[]{:S(2)}) async-start(bf16[32,1,2,4,4,1536]{5,3,2,4,1,0:T(4,128)(2,1)} %bitcast.109), calls=%async_computation.1 | async-start | bytes 6291456 | tf_op jit(solution)/shard_map/all_to_all | solution.py:292
  164.2 3.6 copy-start.1
  191.6 3.8 copy-start.2
  215.6 75.5 %all-to-all-start.2 = ((bf16[32,1,2,4,4,1536]{5,3,4,2,1,0:T(4,128)(2,1)}), bf16[32,1,2,4,4,1536]{5,3,4,2,1,0:T(4,128)(2,1)}, u32[]{:S(2)}, u32[]{:S(2)}) async-start(bf16[32,1,2,4,4,1536]{5,3,4,2,1,0:T(4,128)(2,1)} %pad_maximum_fusion.2), calls=%async_computation.2 | async-start | bytes 6291456 | tf_op jit(solution)/shard_map/all_to_all | solution.py:292
  234.7 60.7 %copy-start.3 = (s32[32,8,128]{2,1,0:T(8,128)S(1)}, s32[32,8,128]{2,1,0:T(8,128)}, u32[]{:S(2)}) copy-start(s32[32,8,128]{2,1,0:T(8,128)} %get-tuple-element.16) | copy-start | bytes 393220
  291.1 75.7 %all-to-all-start.3 = ((bf16[32,1,2,4,4,1536]{5,3,4,2,1,0:T(4,128)(2,1)}), bf16[32,1,2,4,4,1536]{5,3,4,2,1,0:T(4,128)(2,1)}, u32[]{:S(2)}, u32[]{:S(2)}) async-start(bf16[32,1,2,4,4,1536]{5,3,4,2,1,0:T(4,128)(2,1)} %pad_maximum_fusion.3), calls=%async_computation.3 | async-start | bytes 6291456 | tf_op jit(solution)/shard_map/all_to_all | solution.py:292
  348.5 2.9 copy-start
  366.8 81.0 %all-to-all-start.4 = ((bf16[32,1,2,4,4,1664]{5,4,2,3,1,0:T(4,128)(2,1)}), bf16[32,1,2,4,4,1664]{5,4,2,3,1,0:T(4,128)(2,1)S(1)}, u32[]{:S(2)}, u32[]{:S(2)}) async-start(bf16[32,1,2,4,4,1664]{5,4,2,3,1,0:T(4,128)(2,1)} %pad_maximum_fusion), calls=%async_computation.4 | async-start | bytes 6815744 | tf_op jit(solution)/shard_map/all_to_all | solution.py:292
  447.8 76.0 %all-to-all-start.5 = ((bf16[32,1,2,4,4,1536]{5,3,4,2,1,0:T(4,128)(2,1)}), bf16[32,1,2,4,4,1536]{5,3,4,2,1,0:T(4,128)(2,1)}, u32[]{:S(2)}, u32[]{:S(2)}) async-start(bf16[32,1,2,4,4,1536]{5,3,4,2,1,0:T(4,128)(2,1)} %pad_maximum_fusion.1), calls=%async_computation.5 | async-start | bytes 6291456 | tf_op jit(solution)/shard_map/all_to_all | solution.py:292
  523.8 65.2 %all-to-all-start.6 = ((bf16[32,1,1,4,4,1664]{5,4,3,2,1,0:T(4,128)(2,1)}), bf16[32,1,1,4,4,1664]{5,4,3,2,1,0:T(4,128)(2,1)}, u32[]{:S(2)}, u32[]{:S(2)}) async-start(bf16[32,1,1,4,4,1664]{5,4,3,2,1,0:T(4,128)(2,1)} %bitcast.44), calls=%async_computation.6 | async-start | bytes 3407872 | tf_op jit(solution)/shard_map/all_to_all | solution.py:292

commit v3 on v2

--- a/solution.py
+++ b/solution.py
@@ -349,12 +349,13 @@
     far0 = far_part(((q0, 0), (keys, 2), (values, 2)), far_bias(0))
     far1 = far_part(((q12, 0), (kv2, 0), (kv2, 1)), far_bias(1))
     back01_got, back01 = swap(cut(far0, far1), kv1_got)
-    kv0_got, kv0 = swap(cut(keys[:, :1], values[:, :1]), back01_got)
     far2 = far_part(((q12, 1), (kv1, 0), (kv1, 1)), far_bias(2))
-    _, back2 = swap(cut(far2), kv0_got)
-
+    kv0_cut, far2_cut = lax.optimization_barrier((cut(keys[:, :1], values[:, :1]), cut(far2)))
+    kv0_got, kv0 = swap(kv0_cut, back01_got)
     out = near_part(((q_home, 0), (keys, 1), (values, 1)), near_bias(0), back01, 0, 0, planes, None)
     out = near_part(((q_home, 1), (keys, 0), (values, 0)), near_bias(1), back01, 1, 1, planes, out)
+    far2_cut, out = lax.optimization_barrier((far2_cut, out))
+    _, back2 = swap(far2_cut, kv0_got)
     near2 = far_part(((q_home, 2), (kv0, 0), (kv0, 1)), near_bias(2), jnp.float32)
     out = merge_part(near2, back2, 2, out)
     return out.reshape(queries.shape)

time: 604 us -> 584 us (0.967)
  waiting for transfers between devices: 171 us -> 150 us
    all_to_all x7, waiting for transfers between devices: 171 us -> 150 us  [swap_cut(): got = lax.all_to_all(cut, 'seq', split_axis=0, concat_axis=0, tiled=True)]
  transfers between devices with their start and end apart: 7 -> 7, of which waited for: 5 -> 6; matrix products, arithmetic and copies ran while one was open for 27% -> 28% of each run, Pallas kernels for 36% -> 38%
where the time goes in v3:
time: 584 us; the launch traced here: 578 us
  Pallas kernels  223 us (38%)
  waiting for transfers between devices  150 us (26%)
  local copies, waits for them, and re-layouts  115 us (20%)
  matrix products  39.9 us (7%)
  starting transfers between devices  31.2 us (5%)
  other arithmetic  17.5 us (3%)
    all_to_all x7, waiting for transfers between devices, swap_cut(): got = lax.all_to_all(cut, 'seq', split_axis=0, concat_axis=0, tiled=True)  150 us
    pallas_call x1, Pallas kernels, gather_all(): pl.pallas_call(functools.partial(gather_kernel, side, side), out_shape=[j...  117 us
    pallas_call x4, Pallas kernels, far_part(): pl.pallas_call(functools.partial(far_kernel, width // HDIM), grid=(groups...  59.7 us
    reshape x13, local copies, waits for them, and re-layouts, cut_lines(): array.reshape(scenes, lines, planes, size, own, width)  45 us
    pallas_call x2, Pallas kernels, near_part(): pl.pallas_call(functools.partial(near_kernel, width // HDIM), grid=(group...  40.5 us
    all_to_all x7, starting transfers between devices, swap_cut(): got = lax.all_to_all(cut, 'seq', split_axis=0, concat_axis=0, tiled=True)  31.2 us
    reshape x7, local copies, waits for them, and re-layouts, swap(): turned.reshape(-1, turned.shape[2], size * turned.shape[4], turned.shape[5])  24.2 us
    dot_general x1, matrix products, on_device(): jnp.dot(home_rows, key_all.reshape(depth, width), preferred_element_type=...  19.9 us
  transfers between devices with their start and end apart: 7, of which 6 were waited for; matrix products, arithmetic and copies ran while one was open for 28% of the time, Pallas kernels for 38%

profile of v3, /device:TPU:0, one launch (start us, length us, event | category | flops | bytes accessed | tf_op | source)
XLA Modules:
  0.0 577.5 jit_solution(15059282717684157956)
XLA Ops:
  3.9 7.4 %all-to-all-start.1 = ((bf16[32,1,1,4,4,1536]{5,3,4,2,1,0:T(4,128)(2,1)}), bf16[32,1,1,4,4,1536]{5,3,4,2,1,0:T(4,128)(2,1)}, u32[]{:S(2)}, u32[]{:S(2)}) async-start(bf16[32,1,1,4,4,1536]{5,3,4,2,1,0:T(4,128)(2,1)} %bitcast.105), calls=%async_computation.1 | async-start | bytes 3145728 | tf_op jit(solution)/shard_map/all_to_all | solution.py:292
  12.2 116.8 %gather_weights.1 = (s32[32,8,128]{2,1,0:T(8,128)}, bf16[32,96,1536]{2,1,0:T(8,128)(2,1)}, bf16[32,96,1536]{2,1,0:T(8,128)(2,1)}) custom-call(s32[8,128]{1,0:T(8,128)} %pad_bitcast_fusion.code_in, bf16[96,1536]{1,0:T(8,128)(2,1)} %key_in.1, bf16[96,1536]{1,0:T(8,128)(2,1)} %value_in.1), custom_call_target="tpu_custom_call" | custom-call | flops 80000000000 | bytes 20000000 | tf_op jit(solution)/shard_map/gather_weights/pallas_call | solution.py:140
  132.7 4.8 reshape.777
  143.9 19.9 %convolution_convert_fusion.1 = bf16[1536,1536]{0,1:T(8,128)(2,1)S(1)} fusion(bf16[1536,3072]{1,0:T(8,128)(2,1)} %bitcast.133, bf16[3072,1536]{1,0:T(8,128)(2,1)} %bitcast.136), kind=kOutput, calls=%fused_computation.1 | convolution fusion | flops 14497873920 | bytes 23592960 | tf_op jit(solution)/shard_map/dot_general | solution.py:328
  171.3 19.9 %convolution_convert_fusion = bf16[1536,1536]{0,1:T(8,128)(2,1)S(1)} fusion(bf16[1536,3072]{1,0:T(8,128)(2,1)} %bitcast.134, bf16[3072,1536]{1,0:T(8,128)(2,1)} %bitcast.135), kind=kOutput, calls=%fused_computation | convolution fusion | flops 14497873920 | bytes 23592960 | tf_op jit(solution)/shard_map/dot_general | solution.py:330
  195.0 4.2 reshape.782
  206.5 8.7 %all-to-all-done = bf16[32,1,2,4,4,1536]{5,3,2,4,1,0:T(4,128)(2,1)S(1)} async-done(((bf16[32,1,2,4,4,1536]{5,3,2,4,1,0:T(4,128)(2,1)}), bf16[32,1,2,4,4,1536]{5,3,2,4,1,0:T(4,128)(2,1)S(1)}, u32[]{:S(2)}, u32[]{:S(2)}) %all-to-all-start) | async-done | bytes 3145760 | tf_op jit(solution)/shard_map/all_to_all | solution.py:292
  215.3 4.1 all-to-all-start.2
  219.3 3.9 reshape.779
  234.4 56.4 %all-to-all-done.2 = bf16[32,1,2,4,4,1536]{5,3,4,2,1,0:T(4,128)(2,1)} async-done(((bf16[32,1,2,4,4,1536]{5,3,4,2,1,0:T(4,128)(2,1)}), bf16[32,1,2,4,4,1536]{5,3,4,2,1,0:T(4,128)(2,1)}, u32[]{:S(2)}, u32[]{:S(2)}) %all-to-all-start.2) | async-done | bytes 3145760 | tf_op jit(solution)/shard_map/all_to_all | solution.py:292
  290.8 4.2 all-to-all-start.3
  306.0 14.9 %far_slot.5 = bf16[4,1,128,1664]{3,2,1,0:T(8,128)(2,1)} custom-call(bf16[4,1,128,1536]{3,2,1,0:T(8,128)(2,1)} %copy.62.q_ref, bf16[4,3,128,1536]{3,2,1,0:T(8,128)(2,1)} %bitcast.118, bf16[4,3,128,1536]{3,2,1,0:T(8,128)(2,1)} %bitcast.122, f32[4,128,128]{2,1,0:T(8,128)} %get-tuple-element.68.bias_ref), custom_call_target="tpu_custom_call" | custom-call | flops 15099494400 | bytes 6291456 | tf_op jit(solution)/shard_map/far_slot/pallas_call | solution.py:238
  320.8 4.1 copy.63
  333.0 14.9 %far_slot.6 = bf16[4,1,128,1664]{3,2,1,0:T(8,128)(2,1)} custom-call(bf16[4,2,128,1536]{3,2,1,0:T(8,128)(2,1)} %copy.60.q_ref, bf16[4,2,128,1536]{3,2,1,0:T(8,128)(2,1)} %reshape.789.k_ref.v_ref, bf16[4,2,128,1536]{3,2,1,0:T(8,128)(2,1)} %reshape.789.k_ref.v_ref, f32[4,128,128]{2,1,0:T(8,128)} %get-tuple-element.69.bias_ref), custom_call_target="tpu_custom_call" | custom-call | flops 15099494400 | bytes 6291456 | tf_op jit(solution)/shard_map/far_slot/pallas_call | solution.py:238
  350.8 4.0 pad_maximum_fusion
  354.8 11.7 %all-to-all-done.3 = bf16[32,1,2,4,4,1536]{5,3,4,2,1,0:T(4,128)(2,1)} async-done(((bf16[32,1,2,4,4,1536]{5,3,4,2,1,0:T(4,128)(2,1)}), bf16[32,1,2,4,4,1536]{5,3,4,2,1,0:T(4,128)(2,1)}, u32[]{:S(2)}, u32[]{:S(2)}) %all-to-all-start.3) | async-done | bytes 3145760 | tf_op jit(solution)/shard_map/all_to_all | solution.py:292
  366.5 4.2 all-to-all-start.4
  370.6 3.9 reshape.773
  385.7 4.8 copy.48
  390.5 5.9 %reshape.784.k_ref.v_ref = bf16[4,2,128,1536]{3,2,1,0:T(8,128)(2,1)} reshape(bf16[1,4,2,32,4,1536]{5,4,3,2,1,0:T(4,128)(2,1)} %copy.48) | data formatting | bytes 6291456 | tf_op jit(solution)/shard_map/reshape | solution.py:314
  396.4 14.9 %far_slot.4 = bf16[4,1,128,1664]{3,2,1,0:T(8,128)(2,1)} custom-call(bf16[4,2,128,1536]{3,2,1,0:T(8,128)(2,1)} %copy.60.q_ref, bf16[4,2,128,1536]{3,2,1,0:T(8,128)(2,1)} %reshape.784.k_ref.v_ref, bf16[4,2,128,1536]{3,2,1,0:T(8,128)(2,1)} %reshape.784.k_ref.v_ref, f32[4,128,128]{2,1,0:T(8,128)} %get-tuple-element.72.bias_ref), custom_call_target="tpu_custom_call" | custom-call | flops 15099494400 | bytes 6291456 | tf_op jit(solution)/shard_map/far_slot/pallas_call | solution.py:238
  411.3 4.0 copy.61
  415.3 32.4 %all-to-all-done.4 = bf16[32,1,2,4,4,1664]{5,4,2,3,1,0:T(4,128)(2,1)S(1)} async-done(((bf16[32,1,2,4,4,1664]{5,4,2,3,1,0:T(4,128)(2,1)}), bf16[32,1,2,4,4,1664]{5,4,2,3,1,0:T(4,128)(2,1)S(1)}, u32[]{:S(2)}, u32[]{:S(2)}) %all-to-all-start.4) | async-done | bytes 3407904 | tf_op jit(solution)/shard_map/all_to_all | solution.py:292
  447.7 4.3 all-to-all-start.5
  455.1 6.6 %reshape.792.back_ref = bf16[4,2,128,1664]{3,2,1,0:T(8,128)(2,1)} reshape(bf16[1,4,2,32,4,1664]{5,4,3,2,1,0:T(4,128)(2,1)} %copy.58) | data formatting | bytes 6815744 | tf_op jit(solution)/shard_map/reshape | solution.py:314
  461.6 20.2 %near_slot.2.rest_0_ = bf16[4,3,128,1536]{3,2,1,0:T(8,128)(2,1)} custom-call(bf16[4,3,128,1536]{3,2,1,0:T(8,128)(2,1)} %bitcast.114, bf16[4,3,128,1536]{3,2,1,0:T(8,128)(2,1)} %bitcast.119, bf16[4,3,128,1536]{3,2,1,0:T(8,128)(2,1)} %bitcast.123, f32[4,128,128]{2,1,0:T(8,128)} %get-tuple-element.67.bias_ref, bf16[4,2,128,1664]{3,2,1,0:T(8,128)(2,1)} %reshape.792.back_ref), custom_call_target="tpu_custom_call" | custom-call | flops 15099494400 | bytes 6291456 | tf_op jit(solution)/shard_map/near_slot/pallas_call | solution.py:260
  481.9 20.2 %near_slot.3.so_far_ref = bf16[4,3,128,1536]{3,2,1,0:T(8,128)(2,1)} custom-call(bf16[4,3,128,1536]{3,2,1,0:T(8,128)(2,1)} %bitcast.115, bf16[4,3,128,1536]{3,2,1,0:T(8,128)(2,1)} %bitcast.120, bf16[4,3,128,1536]{3,2,1,0:T(8,128)(2,1)} %bitcast.124, f32[4,128,128]{2,1,0:T(8,128)} %get-tuple-element.71.bias_ref, ...), custom_call_target="tpu_custom_call", output_to_operand_aliasing={{}: (5, {})} | custom-call | flops 15099494400 | bytes 6291456 | tf_op jit(solution)/shard_map/near_slot/pallas_call | solution.py:260
  502.1 21.3 %all-to-all-done.5 = bf16[32,1,2,4,4,1536]{5,3,4,2,1,0:T(4,128)(2,1)} async-done(((bf16[32,1,2,4,4,1536]{5,3,4,2,1,0:T(4,128)(2,1)}), bf16[32,1,2,4,4,1536]{5,3,4,2,1,0:T(4,128)(2,1)}, u32[]{:S(2)}, u32[]{:S(2)}) %all-to-all-start.5) | async-done | bytes 3145760 | tf_op jit(solution)/shard_map/all_to_all | solution.py:292
  523.4 4.1 all-to-all-start.6
  533.0 15.0 %far_slot.7.near_ref = f32[4,1,128,1664]{3,2,1,0:T(8,128)} custom-call(bf16[4,3,128,1536]{3,2,1,0:T(8,128)(2,1)} %bitcast.116, bf16[4,2,128,1536]{3,2,1,0:T(8,128)(2,1)} %reshape.791.k_ref.v_ref, bf16[4,2,128,1536]{3,2,1,0:T(8,128)(2,1)} %reshape.791.k_ref.v_ref, f32[4,128,128]{2,1,0:T(8,128)} %get-tuple-element.70.bias_ref), custom_call_target="tpu_custom_call" | custom-call | flops 15099494400 | bytes 6291456 | tf_op jit(solution)/shard_map/far_slot/pallas_call | solution.py:238
  548.0 19.9 %all-to-all-done.6 = bf16[32,1,1,4,4,1664]{5,4,3,2,1,0:T(4,128)(2,1)} async-done(((bf16[32,1,1,4,4,1664]{5,4,3,2,1,0:T(4,128)(2,1)}), bf16[32,1,1,4,4,1664]{5,4,3,2,1,0:T(4,128)(2,1)}, u32[]{:S(2)}, u32[]{:S(2)}) %all-to-all-start.6) | async-done | bytes 1703968 | tf_op jit(solution)/shard_map/all_to_all | solution.py:292
  571.4 5.7 merge_slots.1
  (59 shorter events, 89.5 us)
Async XLA Ops:
  1.9 9.4 %copy-start.4 = (s32[1,4,3,2,2]{1,4,3,2,0:T(2,128)S(1)}, s32[1,4,3,2,2]{1,4,3,2,0:T(2,128)}, u32[]{:S(2)}) copy-start(s32[1,4,3,2,2]{1,4,3,2,0:T(2,128)} %param.9) | copy-start | bytes 580
  3.9 137.0 %all-to-all-start.1 = ((bf16[32,1,1,4,4,1536]{5,3,4,2,1,0:T(4,128)(2,1)}), bf16[32,1,1,4,4,1536]{5,3,4,2,1,0:T(4,128)(2,1)}, u32[]{:S(2)}, u32[]{:S(2)}) async-start(bf16[32,1,1,4,4,1536]{5,3,4,2,1,0:T(4,128)(2,1)} %bitcast.105), calls=%async_computation.1 | async-start | bytes 3145728 | tf_op jit(solution)/shard_map/all_to_all | solution.py:292
  140.9 74.4 %all-to-all-start = ((bf16[32,1,2,4,4,1536]{5,3,2,4,1,0:T(4,128)(2,1)}), bf16[32,1,2,4,4,1536]{5,3,2,4,1,0:T(4,128)(2,1)S(1)}, u32[]{:S(2)}, u32[]{:S(2)}) async-start(bf16[32,1,2,4,4,1536]{5,3,2,4,1,0:T(4,128)(2,1)} %bitcast.109), calls=%async_computation | async-start | bytes 6291456 | tf_op jit(solution)/shard_map/all_to_all | solution.py:292
  163.8 3.6 copy-start.1
  191.3 3.7 copy-start.2
  215.3 75.5 %all-to-all-start.2 = ((bf16[32,1,2,4,4,1536]{5,3,4,2,1,0:T(4,128)(2,1)}), bf16[32,1,2,4,4,1536]{5,3,4,2,1,0:T(4,128)(2,1)}, u32[]{:S(2)}, u32[]{:S(2)}) async-start(bf16[32,1,2,4,4,1536]{5,3,4,2,1,0:T(4,128)(2,1)} %pad_maximum_fusion.3), calls=%async_computation.2 | async-start | bytes 6291456 | tf_op jit(solution)/shard_map/all_to_all | solution.py:292
  234.4 60.7 %copy-start.3 = (s32[32,8,128]{2,1,0:T(8,128)S(1)}, s32[32,8,128]{2,1,0:T(8,128)}, u32[]{:S(2)}) copy-start(s32[32,8,128]{2,1,0:T(8,128)} %get-tuple-element.23) | copy-start | bytes 393220
  290.8 75.7 %all-to-all-start.3 = ((bf16[32,1,2,4,4,1536]{5,3,4,2,1,0:T(4,128)(2,1)}), bf16[32,1,2,4,4,1536]{5,3,4,2,1,0:T(4,128)(2,1)}, u32[]{:S(2)}, u32[]{:S(2)}) async-start(bf16[32,1,2,4,4,1536]{5,3,4,2,1,0:T(4,128)(2,1)} %pad_maximum_fusion.2), calls=%async_computation.3 | async-start | bytes 6291456 | tf_op jit(solution)/shard_map/all_to_all | solution.py:292
  347.9 2.9 copy-start
  366.5 81.2 %all-to-all-start.4 = ((bf16[32,1,2,4,4,1664]{5,4,2,3,1,0:T(4,128)(2,1)}), bf16[32,1,2,4,4,1664]{5,4,2,3,1,0:T(4,128)(2,1)S(1)}, u32[]{:S(2)}, u32[]{:S(2)}) async-start(bf16[32,1,2,4,4,1664]{5,4,2,3,1,0:T(4,128)(2,1)} %pad_maximum_fusion), calls=%async_computation.4 | async-start | bytes 6815744 | tf_op jit(solution)/shard_map/all_to_all | solution.py:292
  447.7 75.8 %all-to-all-start.5 = ((bf16[32,1,2,4,4,1536]{5,3,4,2,1,0:T(4,128)(2,1)}), bf16[32,1,2,4,4,1536]{5,3,4,2,1,0:T(4,128)(2,1)}, u32[]{:S(2)}, u32[]{:S(2)}) async-start(bf16[32,1,2,4,4,1536]{5,3,4,2,1,0:T(4,128)(2,1)} %pad_maximum_fusion.1), calls=%async_computation.5 | async-start | bytes 6291456 | tf_op jit(solution)/shard_map/all_to_all | solution.py:292
  523.4 44.5 %all-to-all-start.6 = ((bf16[32,1,1,4,4,1664]{5,4,3,2,1,0:T(4,128)(2,1)}), bf16[32,1,1,4,4,1664]{5,4,3,2,1,0:T(4,128)(2,1)}, u32[]{:S(2)}, u32[]{:S(2)}) async-start(bf16[32,1,1,4,4,1664]{5,4,3,2,1,0:T(4,128)(2,1)} %bitcast.26), calls=%async_computation.6 | async-start | bytes 3407872 | tf_op jit(solution)/shard_map/all_to_all | solution.py:292
